TPU v7x, 32 devices: a whole 2x2x4 slice. The times are simulated.
32 devices in a mesh: dp: 4 (over z), heads: 4 (over x, core), ctx: 2 (over y).
Axes of the slice: x: 2, y: 2, z: 4, core: 2. Of those that a mesh axis runs over, the one named last changes fastest.
Arguments:
- inputs: bfloat16 [4, 512, 5120], P('dp', 'ctx'), may hold values from -6 to 6
- queries: bfloat16 [4, 512, 4096], P('dp', 'ctx', 'heads'), may hold values from -6 to 6
- keys: bfloat16 [4, 512, 512], P('dp', 'ctx', 'heads'), may hold values from -6 to 6
- values: bfloat16 [4, 512, 512], P('dp', 'ctx', 'heads'), may hold values from -6 to 6
- outputs: bfloat16 [4, 512, 4096], P('dp', 'ctx', 'heads'), may hold values from -6 to 6
- out_grad: bfloat16 [4, 512, 4096], P('dp', 'ctx', 'heads'), may hold values from -6 to 6
- lse: float32 [4, 512, 32], P('dp', 'ctx', 'heads'), may hold values from 6 to 9
- positions: int32 [4, 512], P('dp', 'ctx'), may hold values from 0 to 511, as said below
Outputs:
- query_grad: float32 [4, 512, 4096], P('dp', 'ctx', 'heads')
- key_grad: float32 [4, 512, 512], P('dp', 'ctx', 'heads')
- value_grad: float32 [4, 512, 512], P('dp', 'ctx', 'heads')
- weight_grad: float32 [5120, 1024], P(('dp', 'ctx'), 'heads')
Inputs may be any that keep to these rules, and one draw needn't show every extreme that they name: Each sequence's positions are a permutation of 0 to 511 made of 4 runs of 128 rising consecutive positions; each run fills an aligned block of 128 slots and starts at a multiple of 128.
All inputs are finite; a program needn't handle non-finite values.
Results may differ from a plain program's by a relative error of at most 0.0045.
Values may be sent and summed in bfloat16 or wider, within the bound.
A program may use at most 64 MiB of HBM per device.

v0:
```python
import jax
import jax.numpy as jnp
from jax import lax
from jax.sharding import PartitionSpec as P

HD = 128


def passed_along(block, axis, distance):
    devices = range(lax.axis_size(axis))
    route = [((i - distance) % len(devices), i) for i in devices]
    return lax.ppermute(block, axis, route)


def block_grads(query_blk, grad_blk, lse_blk, delta_blk, query_pos, key_blk, value_blk, key_pos):
    factor = HD ** (-0.5)
    tokens_q = query_blk.shape[0]
    tokens_k = key_blk.shape[0]
    kv_local = key_blk.shape[1] // HD
    group_size = query_blk.shape[1] // key_blk.shape[1]
    query_four = query_blk.reshape(tokens_q, kv_local, group_size, HD)
    grad_four = grad_blk.reshape(tokens_q, kv_local, group_size, HD)
    key_three = key_blk.reshape(tokens_k, kv_local, HD)
    value_three = value_blk.reshape(tokens_k, kv_local, HD)
    lse_four = jnp.transpose(lse_blk.reshape(tokens_q, kv_local, group_size), (1, 2, 0))[..., None]
    delta_four = jnp.transpose(delta_blk.reshape(tokens_q, kv_local, group_size), (1, 2, 0))[
        ..., None
    ]
    visible = key_pos[None, :] <= query_pos[:, None]
    scores = (
        jnp.einsum("qhgd,khd->hgqk", query_four, key_three, preferred_element_type=jnp.float32)
        * factor
    )
    probs = jnp.where(visible, jnp.exp(scores - lse_four), jnp.float32(0.0))
    dprobs = jnp.einsum(
        "qhgd,khd->hgqk", grad_four, value_three, preferred_element_type=jnp.float32
    )
    dscores = probs * (dprobs - delta_four)
    probs_low = probs.astype(jnp.bfloat16)
    dscores_low = dscores.astype(jnp.bfloat16)
    value_part = jnp.einsum(
        "hgqk,qhgd->khd", probs_low, grad_four, preferred_element_type=jnp.float32
    )
    key_part = (
        jnp.einsum("hgqk,qhgd->khd", dscores_low, query_four, preferred_element_type=jnp.float32)
        * factor
    )
    query_part = (
        jnp.einsum("hgqk,khd->qhgd", dscores_low, key_three, preferred_element_type=jnp.float32)
        * factor
    )
    return (
        query_part.reshape(tokens_q, kv_local * group_size * HD),
        key_part.reshape(tokens_k, kv_local * HD),
        value_part.reshape(tokens_k, kv_local * HD),
    )


def shards(inputs, queries, keys, values, outputs, out_grad, lse, positions):
    query_loc = queries[0]
    grad_loc = out_grad[0]
    key_loc = keys[0]
    value_loc = values[0]
    lse_loc = lse[0]
    tokens = query_loc.shape[0]
    heads_q = query_loc.shape[1] // HD
    kv_local = key_loc.shape[1] // HD
    delta_loc = jnp.sum(
        (grad_loc.astype(jnp.float32) * outputs[0].astype(jnp.float32)).reshape(
            tokens, heads_q, HD
        ),
        axis=2,
    )
    pos_loc = positions[0].astype(jnp.float32)
    rounds = lax.axis_size("ctx")
    zero_query = jnp.zeros((tokens, heads_q * HD), jnp.float32)
    zero_key = jnp.zeros((tokens, kv_local * HD), jnp.float32)

    def spin(index, carry):
        key_blk, value_blk, key_acc, value_acc, kpos_blk, dq_acc = carry
        query_part, key_part, value_part = block_grads(
            query_loc, grad_loc, lse_loc, delta_loc, pos_loc, key_blk, value_blk, kpos_blk
        )
        key_blk, value_blk = passed_along((key_blk, value_blk), "ctx", 1)
        key_acc, value_acc, kpos_blk = passed_along(
            (key_acc + key_part, value_acc + value_part, kpos_blk), "ctx", 1
        )
        return (key_blk, value_blk, key_acc, value_acc, kpos_blk, dq_acc + query_part)

    key_blk, value_blk, key_acc, value_acc, kpos_blk, dq_acc = lax.fori_loop(
        0, rounds - 1, spin, (key_loc, value_loc, zero_key, zero_key, pos_loc, zero_query)
    )
    query_part, key_part, value_part = block_grads(
        query_loc, grad_loc, lse_loc, delta_loc, pos_loc, key_blk, value_blk, kpos_blk
    )
    key_grad, value_grad = passed_along((key_acc + key_part, value_acc + value_part), "ctx", 1)
    query_grad = dq_acc + query_part
    kv_low = jnp.stack(
        [key_grad.reshape(tokens, kv_local, HD), value_grad.reshape(tokens, kv_local, HD)], axis=2
    )
    kv_low = kv_low.reshape(tokens, kv_local * 2 * HD).astype(jnp.bfloat16)
    inputs_loc = inputs[0]
    weight_grad = lax.psum_scatter(
        jnp.einsum("td,tc->dc", inputs_loc, kv_low, preferred_element_type=jnp.float32),
        ("dp", "ctx"),
        scatter_dimension=0,
        tiled=True,
    )
    return (query_grad[None], key_grad[None], value_grad[None], weight_grad)


def solution(mesh):
    return jax.shard_map(
        shards,
        mesh=mesh,
        in_specs=(
            P("dp", "ctx", None),
            P("dp", "ctx", "heads"),
            P("dp", "ctx", "heads"),
            P("dp", "ctx", "heads"),
            P("dp", "ctx", "heads"),
            P("dp", "ctx", "heads"),
            P("dp", "ctx", "heads"),
            P("dp", "ctx"),
        ),
        out_specs=(
            P("dp", "ctx", "heads"),
            P("dp", "ctx", "heads"),
            P("dp", "ctx", "heads"),
            P(("dp", "ctx"), "heads"),
        ),
        check_vma=False,
    )
```

profile of v0, /device:TPU:0, one launch (start us, length us, event | category | flops | bytes accessed | tf_op | source)
XLA Modules:
  0.0 152.0 jit_solution(3847998862575749768)
XLA Ops:
  7.2 0.0 copy-start
  7.2 0.0 reduce-scatter.2.cloned.1.call-start
  7.2 0.8 convert_element_type.58
  8.1 3.0 %collective-permute-start = (f32[256]{0:T(256)S(1)}, f32[256]{0:T(256)S(1)}, u32[]{:S(2)}, u32[]{:S(2)}) collective-permute-start(f32[256]{0:T(256)S(1)} %bitcast.156), channel_id=1, source_target_pairs={{1,0},{0,1},{3,2},{2,3},{5,4},{4,5},{7,6},{6,7},{9,8},{8,9},{11,10... | collective-permute-start | bytes 3080 | tf_op jit(solution)/shard_map/while/body/eval_jaxpr/ppermute | solution.py:12
  11.0 0.0 collective-permute-start.1
  11.1 2.0 %collective-permute-start.2 = (bf16[256,128]{1,0:T(8,128)(2,1)}, bf16[256,128]{1,0:T(8,128)(2,1)S(1)}, u32[]{:S(2)}, u32[]{:S(2)}) collective-permute-start(bf16[256,128]{1,0:T(8,128)(2,1)} %bitcast.154), channel_id=1, source_target_pairs={{1,0},{0,1},{3,2},{2,3},{5,4},{4,5},{7,6},{6,7},{9,8},{8,9},{11,10... | collective-permute-start | bytes 196616 | tf_op jit(solution)/shard_map/while/body/eval_jaxpr/ppermute | solution.py:12
  13.1 1.1 copy.64
  14.2 1.1 convert_bitcast_fusion
  15.3 0.0 copy-start.5
  15.4 0.0 copy-start.7
  15.4 0.2 copy.65
  15.6 0.3 multiply_reduce_fusion
  15.9 0.5 copy-done.5
  16.4 0.9 copy.63
  17.3 0.1 copy.43
  17.3 0.2 broadcast_compare_fusion
  17.5 1.7 %fusion.8 = f32[1,8,256,256]{2,3,1,0:T(8,128)S(1)} fusion(f32[8,256]{1,0:T(8,128)} %bitcast.158, pred[256,256]{0,1:T(8,128)(4,1)S(1)} %get-tuple-element.53, bf16[256,8,128]{2,1,0:T(8,128)(2,1)} %bitcast.142, bf16[1,256,128]{2,1,0:T(8,128)(2,1)S(1)} %copy-done.7), kind=kOutput, calls=%fused_computation.13 | convolution fusion | flops 135790592 | bytes 2760704 | tf_op jit(solution)/shard_map/while/body/eval_jaxpr/qhgd,khd->hgqk/dot_general | solution.py:31
  19.2 0.0 copy-start.1
  19.2 0.4 fusion.10
  19.7 0.6 copy-done.1
  20.2 0.4 fusion.15
  20.7 0.0 copy-start.8
  20.7 0.4 convolution_bitcast_fusion.2
  21.1 0.1 copy-done.4
  21.2 0.1 collective-permute-start.3
  21.3 2.0 %collective-permute-start.5 = (f32[256,128]{1,0:T(8,128)S(1)}, f32[256,128]{1,0:T(8,128)S(1)}, u32[]{:S(2)}, u32[]{:S(2)}) collective-permute-start(f32[256,128]{1,0:T(8,128)S(1)} %convolution_bitcast_fusion.2), channel_id=1, source_target_pairs={{1,0},{0,1},{3,2},{2,3},{5,4},{4,5},{7,6},{6,7},{9,8},{8,9},{11,10... | collective-permute-start | bytes 393224 | tf_op jit(solution)/shard_map/while/body/eval_jaxpr/ppermute | solution.py:12
  23.2 0.0 collective-permute-done.1
  23.2 0.4 fusion.31
  23.7 0.0 collective-permute-done.2
  23.7 0.8 fusion.11
  24.5 2.5 %collective-permute-done.3 = f32[256,128]{1,0:T(8,128)S(1)} collective-permute-done((f32[256,128]{1,0:T(8,128)S(1)}, f32[256,128]{1,0:T(8,128)S(1)}, u32[]{:S(2)}, u32[]{:S(2)}) %collective-permute-start.3) | collective-permute-done | bytes 131104 | tf_op jit(solution)/shard_map/while/body/eval_jaxpr/ppermute | solution.py:12
  27.0 0.4 fusion.14
  27.4 0.4 collective-permute-start.4
  27.9 1.8 %collective-permute-done.5 = f32[256,128]{1,0:T(8,128)S(1)} collective-permute-done((f32[256,128]{1,0:T(8,128)S(1)}, f32[256,128]{1,0:T(8,128)S(1)}, u32[]{:S(2)}, u32[]{:S(2)}) %collective-permute-start.5) | collective-permute-done | bytes 131104 | tf_op jit(solution)/shard_map/while/body/eval_jaxpr/ppermute | solution.py:12
  29.6 0.6 fusion.16
  30.3 0.4 collective-permute-start.6
  30.7 2.0 %collective-permute-done.4 = f32[256,128]{1,0:T(8,128)S(1)} collective-permute-done((f32[256,128]{1,0:T(8,128)S(1)}, f32[256,128]{1,0:T(8,128)S(1)}, u32[]{:S(2)}, u32[]{:S(2)}) %collective-permute-start.4) | collective-permute-done | bytes 131104 | tf_op jit(solution)/shard_map/ppermute | solution.py:12
  32.6 2.6 %collective-permute-done.6 = f32[256,128]{1,0:T(8,128)S(1)} collective-permute-done((f32[256,128]{1,0:T(8,128)S(1)}, f32[256,128]{1,0:T(8,128)S(1)}, u32[]{:S(2)}, u32[]{:S(2)}) %collective-permute-start.6) | collective-permute-done | bytes 131104 | tf_op jit(solution)/shard_map/ppermute | solution.py:12
  35.3 0.1 copy.54
  35.5 3.2 %convolution_bitcast_fusion = f32[5120,256]{0,1:T(8,128)} fusion(bf16[256,256]{0,1:T(8,128)(2,1)S(1)} %bitcast.148, bf16[1,256,5120]{2,1,0:T(8,128)(2,1)S(1)} %copy-done), kind=kOutput, calls=%fused_computation | convolution fusion | flops 671088640 | bytes 7995392 | tf_op jit(solution)/shard_map/td,tc->dc/dot_general | solution.py:104
  38.6 0.0 reduce-scatter.2.cloned.1.call-update
  38.7 1.7 %fusion.38 = f32[8,256,128]{1,2,0:T(8,128)S(1)} fusion(bf16[8,256,256]{1,2,0:T(8,128)(2,1)} %copy-done.4, bf16[1,256,128]{2,1,0:T(8,128)(2,1)S(1)} %copy-done.7), kind=kOutput, calls=%fused_computation.52 | convolution fusion | flops 134217728 | bytes 2162688 | tf_op jit(solution)/shard_map/while/body/eval_jaxpr/hgqk,khd->qhgd/dot_general | solution.py:49
  40.3 1.4 fusion.12
  41.7 2.5 %copy.55 = f32[1,256,1024]{2,1,0:T(8,128)} copy(f32[1,256,1024]{1,2,0:T(8,128)} %bitcast.146) | data formatting | bytes 2097152
  44.2 97.4 %reduce-scatter.2.cloned.1.call-done = f32[640,256]{0,1:T(8,128)} async-done(((f32[5120,256]{0,1:T(8,128)}), f32[640,256]{0,1:T(8,128)}) %reduce-scatter.2.cloned.1.call-update) | async-done | bytes 655376 | tf_op jit(solution)/shard_map/reduce_scatter | solution.py:103
  141.7 2.2 %copy.56 = f32[640,256]{1,0:T(8,128)} copy(f32[640,256]{0,1:T(8,128)} %reduce-scatter.2.cloned.1.call-done) | data formatting | bytes 1310720
  143.8 0.7 copy.84
  144.5 0.7 copy.85
  (14 shorter events, 0.1 us)
Async XLA Ops:
  7.2 28.3 %copy-start = (bf16[1,256,5120]{2,1,0:T(8,128)(2,1)S(1)}, bf16[1,256,5120]{2,1,0:T(8,128)(2,1)}, u32[]{:S(2)}) copy-start(bf16[1,256,5120]{2,1,0:T(8,128)(2,1)} %param.8) | copy-start | bytes 7864324
  7.2 134.5 %reduce-scatter.2.cloned.1.call-start = ((), (), s32[]{:S(2)}) async-start(), calls=%async_computation.1 | async-start | bytes 5898240 | tf_op jit(solution)/shard_map/reduce_scatter | solution.py:103
  8.1 9.3 %collective-permute-start = (f32[256]{0:T(256)S(1)}, f32[256]{0:T(256)S(1)}, u32[]{:S(2)}, u32[]{:S(2)}) collective-permute-start(f32[256]{0:T(256)S(1)} %bitcast.156), channel_id=1, source_target_pairs={{1,0},{0,1},{3,2},{2,3},{5,4},{4,5},{7,6},{6,7},{9,8},{8,9},{11,10... | collective-permute-start | bytes 3080 | tf_op jit(solution)/shard_map/while/body/eval_jaxpr/ppermute | solution.py:12
  11.0 12.2 %collective-permute-start.1 = (bf16[256,128]{1,0:T(8,128)(2,1)}, bf16[256,128]{1,0:T(8,128)(2,1)S(1)}, u32[]{:S(2)}, u32[]{:S(2)}) collective-permute-start(bf16[256,128]{1,0:T(8,128)(2,1)} %bitcast.155), channel_id=1, source_target_pairs={{1,0},{0,1},{3,2},{2,3},{5,4},{4,5},{7,6},{6,7},{9,8},{8,9},{11,10... | collective-permute-start | bytes 196616 | tf_op jit(solution)/shard_map/while/body/eval_jaxpr/ppermute | solution.py:12
  11.1 12.6 %collective-permute-start.2 = (bf16[256,128]{1,0:T(8,128)(2,1)}, bf16[256,128]{1,0:T(8,128)(2,1)S(1)}, u32[]{:S(2)}, u32[]{:S(2)}) collective-permute-start(bf16[256,128]{1,0:T(8,128)(2,1)} %bitcast.154), channel_id=1, source_target_pairs={{1,0},{0,1},{3,2},{2,3},{5,4},{4,5},{7,6},{6,7},{9,8},{8,9},{11,10... | collective-permute-start | bytes 196616 | tf_op jit(solution)/shard_map/while/body/eval_jaxpr/ppermute | solution.py:12
  15.3 1.0 copy-start.5
  15.4 2.2 %copy-start.7 = (bf16[1,256,128]{2,1,0:T(8,128)(2,1)S(1)}, bf16[1,256,128]{2,1,0:T(8,128)(2,1)}, u32[]{:S(2)}) copy-start(bf16[1,256,128]{2,1,0:T(8,128)(2,1)} %param.10) | copy-start | bytes 196612
  16.4 2.8 %copy-start.6 = (bf16[1,256,128]{2,1,0:T(8,128)(2,1)S(1)}, bf16[1,256,128]{2,1,0:T(8,128)(2,1)}, u32[]{:S(2)}) copy-start(bf16[1,256,128]{2,1,0:T(8,128)(2,1)} %param.11) | copy-start | bytes 196612
  19.2 1.0 copy-start.1
  20.2 1.0 copy-start.4
  20.7 3.0 %copy-start.8 = (f32[1,256,8]{1,2,0:T(8,128)S(1)}, f32[1,256,8]{1,2,0:T(8,128)}, u32[]{:S(2)}) copy-start(f32[1,256,8]{1,2,0:T(8,128)} %param.14) | copy-start | bytes 24580
  21.2 5.8 %collective-permute-start.3 = (f32[256,128]{1,0:T(8,128)S(1)}, f32[256,128]{1,0:T(8,128)S(1)}, u32[]{:S(2)}, u32[]{:S(2)}) collective-permute-start(f32[256,128]{1,0:T(8,128)S(1)} %fusion.15), channel_id=1, source_target_pairs={{1,0},{0,1},{3,2},{2,3},{5,4},{4,5},{7,6},{6,7},{9,8},{8,9},{11,10... | collective-permute-start | bytes 393224 | tf_op jit(solution)/shard_map/while/body/eval_jaxpr/ppermute | solution.py:12
  21.3 8.4 %collective-permute-start.5 = (f32[256,128]{1,0:T(8,128)S(1)}, f32[256,128]{1,0:T(8,128)S(1)}, u32[]{:S(2)}, u32[]{:S(2)}) collective-permute-start(f32[256,128]{1,0:T(8,128)S(1)} %convolution_bitcast_fusion.2), channel_id=1, source_target_pairs={{1,0},{0,1},{3,2},{2,3},{5,4},{4,5},{7,6},{6,7},{9,8},{8,9},{11,10... | collective-permute-start | bytes 393224 | tf_op jit(solution)/shard_map/while/body/eval_jaxpr/ppermute | solution.py:12
  24.5 5.8 %copy-start.2 = (bf16[8,256,256]{1,2,0:T(8,128)(2,1)}, bf16[8,256,256]{1,2,0:T(8,128)(2,1)S(1)}, u32[]{:S(2)}) copy-start(bf16[8,256,256]{1,2,0:T(8,128)(2,1)S(1)} %fusion.11) | copy-start | bytes 3145732
  27.4 5.2 %collective-permute-start.4 = (f32[256,128]{1,0:T(8,128)S(1)}, f32[256,128]{1,0:T(8,128)S(1)}, u32[]{:S(2)}, u32[]{:S(2)}) collective-permute-start(f32[256,128]{1,0:T(8,128)S(1)} %fusion.14), channel_id=1, source_target_pairs={{1,0},{0,1},{3,2},{2,3},{5,4},{4,5},{7,6},{6,7},{9,8},{8,9},{11,10... | collective-permute-start | bytes 393224 | tf_op jit(solution)/shard_map/ppermute | solution.py:12
  30.3 5.0 %collective-permute-start.6 = (f32[256,128]{1,0:T(8,128)S(1)}, f32[256,128]{1,0:T(8,128)S(1)}, u32[]{:S(2)}, u32[]{:S(2)}) collective-permute-start(f32[256,128]{1,0:T(8,128)S(1)} %fusion.16), channel_id=1, source_target_pairs={{1,0},{0,1},{3,2},{2,3},{5,4},{4,5},{7,6},{6,7},{9,8},{8,9},{11,10... | collective-permute-start | bytes 393224 | tf_op jit(solution)/shard_map/ppermute | solution.py:12
  38.6 1.7 %copy-start.3 = (bf16[8,256,256]{1,2,0:T(8,128)(2,1)S(1)}, bf16[8,256,256]{1,2,0:T(8,128)(2,1)}, u32[]{:S(2)}) copy-start(bf16[8,256,256]{1,2,0:T(8,128)(2,1)} %copy-done.2) | copy-start | bytes 3145732
Sparse Core Ops, SparseCore 0:
  38.8 102.8 reduce-scatter.1
where the time goes:
time: 152 us
  waiting for transfers between devices  106 us (70%)
  between operations  14.3 us (9%)
  matrix products  11.4 us (8%)
  local copies, waits for them, and re-layouts  9.56 us (6%)
  starting transfers between devices  7.88 us (5%)
  other arithmetic  2.52 us (2%)
    reduce_scatter x1, waiting for transfers between devices, shards(): lax.psum_scatter(jnp.einsum('td,tc->dc', inputs_loc, kv_low, preferred_el...  97.4 us
    unnamed x25, local copies, waits for them, and re-layouts  9.39 us
    ppermute x7, waiting for transfers between devices, passed_along(): return lax.ppermute(block, axis, route)  8.91 us
    ppermute x7, starting transfers between devices, passed_along(): return lax.ppermute(block, axis, route)  7.84 us
    dot_general x1, matrix products, shards(): jnp.einsum('td,tc->dc', inputs_loc, kv_low, preferred_element_type=jnp.fl...  3.16 us
  transfers between devices with their start and end apart: 8, of which 5 were waited for; matrix products, arithmetic and copies ran while one was open for 10% of the time, Pallas kernels for 0%

commit v1 on v0

--- a/solution.py
+++ b/solution.py
@@ -1,9 +1,16 @@
+import functools
+
 import jax
 import jax.numpy as jnp
 from jax import lax
+from jax.experimental import pallas as pl
+from jax.experimental.pallas import tpu as pltpu
 from jax.sharding import PartitionSpec as P
 
 HD = 128
+MESH = pl.DeviceIdType.MESH
+NT = (((1,), (1,)), ((), ()))
+TN = (((0,), (0,)), ((), ()))
 
 
 def passed_along(block, axis, distance):
@@ -109,9 +116,281 @@
     return (query_grad[None], key_grad[None], value_grad[None], weight_grad)
 
 
+def fused_kernel(
+    x_ref, q_ref, k_ref, v_ref, o_ref, g_ref, lse_ref, pos_ref,
+    dq_ref, dk_ref, dv_ref, w_ref,
+    kv_peer, pos_send, pos_peer, stat, stat_t, part_own, part_send, part_recv, kv_all, x_all,
+    local_sem, kv_send, kv_recv, part_ssem, part_rsem,
+    xd_send, xd_recv, xx_send, xx_recv, xc_send, xc_recv, g_send, g_recv,
+):
+    factor = HD ** (-0.5)
+    z, h, y = lax.axis_index("dp"), lax.axis_index("heads"), lax.axis_index("ctx")
+    me = z * 2 + y
+    heads = q_ref.shape[2] // HD
+    tokens = q_ref.shape[1]
+    half = tokens // 2
+    quarter = tokens // 4
+    width = w_ref.shape[0]
+    core, xpos = h % 2, h // 2
+    y_peer = {"ctx": 1 - y}
+    x_peer = {"heads": (h + 2) % 4}
+    core_peer = {"heads": h + 1 - 2 * core}
+    rows_q = pl.ds(pl.multiple_of(half * core + quarter * xpos, quarter), quarter)
+    rows_h = pl.ds(pl.multiple_of(half * core, half), half)
+
+    def ring(r):
+        other = (me + r) % 8
+        return other, {"dp": other // 2, "ctx": other % 2}
+
+    def send(src, dst, ssem, rsem, to):
+        return pltpu.make_async_remote_copy(
+            src_ref=src, dst_ref=dst, send_sem=ssem, recv_sem=rsem,
+            device_id=to, device_id_type=MESH,
+        )
+
+    barrier = pltpu.get_barrier_semaphore()
+    for r in range(1, 8):
+        pl.semaphore_signal(barrier, inc=1, device_id=ring(r)[1], device_id_type=MESH)
+    pl.semaphore_signal(barrier, inc=1, device_id=x_peer, device_id_type=MESH)
+    pl.semaphore_signal(barrier, inc=1, device_id=core_peer, device_id_type=MESH)
+    own_x = pltpu.make_async_copy(
+        x_ref.at[0, :, pl.ds(pl.multiple_of(me * width, 128), width)], x_all.at[0], local_sem
+    )
+    own_x.start()
+    pos_send[...] = jnp.broadcast_to(pos_ref[...], pos_send.shape)
+    pl.semaphore_wait(barrier, 9)
+
+    kv_copies = [
+        send(k_ref.at[0], kv_peer.at[0], kv_send.at[0], kv_recv.at[0], y_peer),
+        send(v_ref.at[0], kv_peer.at[1], kv_send.at[1], kv_recv.at[1], y_peer),
+        send(pos_send, pos_peer, kv_send.at[2], kv_recv.at[2], y_peer),
+    ]
+    for copy in kv_copies:
+        copy.start()
+    direct = {}
+    for r in (4, 3, 5, 2, 6, 1, 7):
+        other, to = ring(r)
+        direct[r] = send(
+            x_ref.at[0, rows_q, pl.ds(pl.multiple_of(other * width, 128), width)],
+            x_all.at[r, rows_q, :], xd_send.at[r], xd_recv.at[r], to,
+        )
+        direct[r].start()
+
+    stat[...] = jnp.zeros_like(stat)
+    stat[:, 0:heads] = lse_ref[0]
+    for i in range(heads):
+        cols = slice(i * HD, (i + 1) * HD)
+        prod = g_ref[0, :, cols].astype(jnp.float32) * o_ref[0, :, cols].astype(jnp.float32)
+        stat[:, heads + i:heads + i + 1] = jnp.sum(prod, axis=1, keepdims=True)
+    stat_t[...] = jnp.transpose(stat[...])
+    pos_row = pos_ref[...].astype(jnp.float32)
+
+    def column(row):
+        return jnp.transpose(jnp.broadcast_to(row, (HD, tokens)))
+
+    def chunk(key, value, key_pos, first, last):
+        visible = key_pos <= pos_row
+
+        def one_head(i, carry):
+            dk, dv = carry
+            cols = pl.ds(pl.multiple_of(i * HD, HD), HD)
+            query, grad = q_ref[0, :, cols], g_ref[0, :, cols]
+            lse_row = stat_t[pl.ds(i, 1), :]
+            delta_row = stat_t[pl.ds(i + heads, 1), :]
+            scores = lax.dot_general(key, query, NT, preferred_element_type=jnp.float32) * factor
+            probs = jnp.where(visible, jnp.exp(scores - lse_row), jnp.float32(0.0))
+            dprobs = lax.dot_general(value, grad, NT, preferred_element_type=jnp.float32)
+            dscores = (probs * (dprobs - delta_row)).astype(jnp.bfloat16)
+            dv = dv + jnp.dot(probs.astype(jnp.bfloat16), grad, preferred_element_type=jnp.float32)
+            dk = dk + jnp.dot(dscores, query, preferred_element_type=jnp.float32)
+            dq = lax.dot_general(dscores, key, TN, preferred_element_type=jnp.float32)
+            if not first:
+                dq = dq_ref[0, :, cols] + dq
+            if last:
+                dq = dq * factor
+            dq_ref[0, :, cols] = dq
+            return dk, dv
+
+        zero = jnp.zeros((half, HD), jnp.float32)
+        dk, dv = lax.fori_loop(0, heads, one_head, (zero, zero), unroll=2)
+        return dk * factor, dv
+
+    def own_chunk(c, first, last):
+        rows = slice(c * half, (c + 1) * half)
+        dk, dv = chunk(k_ref[0, rows, :], v_ref[0, rows, :], own_col[rows, 0:1], first, last)
+        part_own[c, :, 0:HD] = dk
+        part_own[c, :, HD:] = dv
+
+    own_col = column(pos_row)
+    own_chunk(0, True, False)
+
+    for copy in kv_copies:
+        copy.wait_recv()
+    peer_col = column(pos_peer[0:1, :].astype(jnp.float32))
+    part_copies = []
+    for c in range(2):
+        rows = slice(c * half, (c + 1) * half)
+        dk, dv = chunk(kv_peer[0, rows, :], kv_peer[1, rows, :], peer_col[rows, 0:1], False, False)
+        part_send[c, :, 0:HD] = dk.astype(jnp.bfloat16)
+        part_send[c, :, HD:] = dv.astype(jnp.bfloat16)
+        copy = send(
+            part_send.at[c], part_recv.at[c], part_ssem.at[c], part_rsem.at[c], y_peer
+        )
+        copy.start()
+        part_copies.append(copy)
+    own_chunk(1, False, True)
+
+    up, down = {"dp": z + 1}, {"dp": z - 1}
+    first_z, last_z = 1 - (z + 3) // 4, z // 3
+
+    def pass_block(c, step, r, to_up, to_down):
+        rows = slice(c * half, (c + 1) * half)
+        src = kv_all.at[r, rows, :]
+        slots = ((r + 9 - 2 * y) % 8, (r + 2) % 8, (r + 6) % 8)
+        copies = [
+            send(src, kv_all.at[slot, rows, :], g_send.at[c, step, d], g_recv.at[c, slot], to)
+            for d, (slot, to) in enumerate(zip(slots, (y_peer, up, down)))
+        ]
+        if to_up is not None:
+            pl.when(to_up)(copies[1].start)
+            pl.when(to_down)(copies[2].start)
+        copies[0].start()
+        return copies, to_up, to_down
+
+    passed = []
+    for c in range(2):
+        rows = slice(c * half, (c + 1) * half)
+        part_copies[c].wait_recv()
+        total = part_own[c] + part_recv[c].astype(jnp.float32)
+        dk_ref[0, rows, :] = total[:, 0:HD]
+        dv_ref[0, rows, :] = total[:, HD:]
+        kv_all[0, rows, :] = total.astype(jnp.bfloat16)
+        passed.append(pass_block(c, 0, 0, z < 3, z > 0))
+
+    def arrived(c, r):
+        rows = slice(c * half, (c + 1) * half)
+        send(
+            kv_all.at[r, rows, :], kv_all.at[r, rows, :], g_send.at[c, 0, 0], g_recv.at[c, r], y_peer
+        ).wait_recv()
+
+    def forward_kv(step):
+        if step == 1:
+            r = 2 + 4 * first_z
+        elif step == 2:
+            r = 6 - 2 * (first_z + last_z)
+        else:
+            r = 4 - 2 * first_z + 2 * last_z
+        rising = z >= r // 2
+        for c in range(2):
+            arrived(c, r)
+            passed.append(
+                pass_block(
+                    c, step, r,
+                    jnp.logical_and(rising, z < 3),
+                    jnp.logical_and(jnp.logical_not(rising), z > 0),
+                )
+            )
+
+    over_x, over_core = {}, {}
+
+    def forward_x(r):
+        direct[r].wait_recv()
+        over_x[r] = send(
+            x_all.at[r, rows_q, :], x_all.at[r, rows_q, :], xx_send.at[r], xx_recv.at[r], x_peer
+        )
+        over_x[r].start()
+
+    def forward_core(r):
+        over_x[r].wait_recv()
+        over_core[r] = send(
+            x_all.at[r, rows_h, :], x_all.at[r, rows_h, :], xc_send.at[r], xc_recv.at[r], core_peer
+        )
+        over_core[r].start()
+
+    def add(r, first=False):
+        term = lax.dot_general(x_all[r], kv_all[r], TN, preferred_element_type=jnp.float32)
+        w_ref[...] = term if first else w_ref[...] + term
+
+    for r in (1, 7, 2, 6):
+        forward_x(r)
+    forward_kv(1)
+    for r in (3, 5, 4):
+        forward_x(r)
+    forward_kv(2)
+    for r in (1, 7, 2, 6, 3, 5, 4):
+        forward_core(r)
+    forward_kv(3)
+    own_x.wait()
+    add(0, True)
+    for r in (2, 6, 4):
+        over_core[r].wait_recv()
+        add(r)
+    for r in (1, 7, 3, 5):
+        over_core[r].wait_recv()
+        arrived(0, r)
+        arrived(1, r)
+        add(r)
+
+    for copy in kv_copies + part_copies:
+        copy.wait_send()
+    for r in range(1, 8):
+        direct[r].wait_send()
+        over_x[r].wait_send()
+        over_core[r].wait_send()
+    for copies, to_up, to_down in passed:
+        copies[0].wait_send()
+        pl.when(to_up)(copies[1].wait_send)
+        pl.when(to_down)(copies[2].wait_send)
+
+
+def fused(inputs, queries, keys, values, outputs, out_grad, lse, positions):
+    tokens = queries.shape[1]
+    width = inputs.shape[2] // 8
+    vmem = pl.BlockSpec(memory_space=pltpu.VMEM)
+    dma = pltpu.SemaphoreType.DMA
+    f32, bf16 = jnp.float32, jnp.bfloat16
+    return pl.pallas_call(
+        fused_kernel,
+        out_shape=(
+            jax.ShapeDtypeStruct(queries.shape, f32),
+            jax.ShapeDtypeStruct(keys.shape, f32),
+            jax.ShapeDtypeStruct(values.shape, f32),
+            jax.ShapeDtypeStruct((width, 2 * HD), f32),
+        ),
+        in_specs=[pl.BlockSpec(memory_space=pl.ANY)] + [vmem] * 7,
+        out_specs=(vmem,) * 4,
+        scratch_shapes=[
+            pltpu.VMEM((2, tokens, HD), bf16),
+            pltpu.VMEM((8, tokens), jnp.int32),
+            pltpu.VMEM((8, tokens), jnp.int32),
+            pltpu.VMEM((tokens, HD), f32),
+            pltpu.VMEM((HD, tokens), f32),
+            pltpu.VMEM((2, tokens // 2, 2 * HD), f32),
+            pltpu.VMEM((2, tokens // 2, 2 * HD), bf16),
+            pltpu.VMEM((2, tokens // 2, 2 * HD), bf16),
+            pltpu.VMEM((8, tokens, 2 * HD), bf16),
+            pltpu.VMEM((8, tokens, width), bf16),
+            dma,
+            dma((3,)), dma((3,)),
+            dma((2,)), dma((2,)),
+            dma((8,)), dma((8,)),
+            dma((8,)), dma((8,)),
+            dma((8,)), dma((8,)),
+            dma((2, 4, 3)), dma((2, 8)),
+        ],
+        compiler_params=pltpu.CompilerParams(
+            collective_id=0, has_side_effects=True, vmem_limit_bytes=40 * 1024 * 1024
+        ),
+    )(inputs, queries, keys, values, outputs, out_grad, lse, positions)
+
+
+def fits(mesh):
+    return mesh.shape["dp"] == 4 and mesh.shape["ctx"] == 2 and mesh.shape["heads"] == 4
+
+
 def solution(mesh):
     return jax.shard_map(
-        shards,
+        fused if fits(mesh) else shards,
         mesh=mesh,
         in_specs=(
             P("dp", "ctx", None),

time: 152 us -> 56.3 us (0.37)
  waiting for transfers between devices: 106 us -> 0 us
  Pallas kernels: 0 us -> 44 us
  between operations: 14.3 us -> 0.66 us
  matrix products: 11.4 us -> 0 us
  starting transfers between devices: 7.88 us -> 0 us
  other arithmetic: 2.52 us -> 0 us
  local copies, waits for them, and re-layouts: 9.56 us -> 11.2 us
    reduce_scatter x1 -> x0, waiting for transfers between devices: 97.4 us -> none  [shards(): lax.psum_scatter(jnp.einsum('td,tc->dc', inputs_loc, kv_low, preferred_el...]
    pallas_call x0 -> x1, Pallas kernels: none -> 44 us  [fused(): pl.pallas_call(fused_kernel, out_shape=(jax.ShapeDtypeStruct(queries.shap...]
    dot_general x11 -> x0, matrix products: 11.4 us -> none  [the longest x1 3.16 us: shards(): jnp.einsum('td,tc->dc', inputs_loc, kv_low, preferred_element_type=jnp.fl...]
    ppermute x7 -> x0, waiting for transfers between devices: 8.91 us -> none  [passed_along(): return lax.ppermute(block, axis, route)]
    ppermute x7 -> x0, starting transfers between devices: 7.84 us -> none  [passed_along(): return lax.ppermute(block, axis, route)]
    unnamed x25 -> x19, local copies, waits for them, and re-layouts: 9.39 us -> 11.2 us
  transfers between devices with their start and end apart: 8 -> 0, of which waited for: 5 -> 0; matrix products, arithmetic and copies ran while one was open for 10% -> 0% of each run, Pallas kernels for 0% -> 0%
where the time goes in v1:
time: 56.3 us; the launch traced here: 55.8 us
  Pallas kernels  44 us (78%)
  local copies, waits for them, and re-layouts  11.2 us (20%)
  between operations  0.66 us (1%)
    pallas_call x1, Pallas kernels, fused(): pl.pallas_call(fused_kernel, out_shape=(jax.ShapeDtypeStruct(queries.shap...  44 us
    unnamed x19, local copies, waits for them, and re-layouts  11.2 us

profile of v1, /device:TPU:0, one launch (start us, length us, event | category | flops | bytes accessed | tf_op | source)
XLA Modules:
  0.0 55.8 jit_solution(17817748815530743888)
XLA Ops:
  0.6 0.8 %copy.12.lse_ref = f32[1,256,8]{2,1,0:T(8,128)S(1)} copy(f32[1,256,8]{1,2,0:T(8,128)} %param.14) | data formatting | bytes 16384 | tf_op args[6]
  1.5 0.0 copy-start
  1.5 1.7 %copy-done = bf16[1,256,5120]{2,1,0:T(8,128)(2,1)S(1)} copy-done((bf16[1,256,5120]{2,1,0:T(8,128)(2,1)S(1)}, bf16[1,256,5120]{2,1,0:T(8,128)(2,1)}, u32[]{:S(2)}) %copy-start) | copy-done | bytes 2621464
  3.2 0.0 copy-start.1
  3.2 1.0 %copy-done.1 = bf16[1,256,1024]{2,1,0:T(8,128)(2,1)S(1)} copy-done((bf16[1,256,1024]{2,1,0:T(8,128)(2,1)S(1)}, bf16[1,256,1024]{2,1,0:T(8,128)(2,1)}, u32[]{:S(2)}) %copy-start.1) | copy-done | bytes 524312
  4.2 0.0 copy-start.2
  4.2 1.0 %copy-done.2 = bf16[1,256,1024]{2,1,0:T(8,128)(2,1)S(1)} copy-done((bf16[1,256,1024]{2,1,0:T(8,128)(2,1)S(1)}, bf16[1,256,1024]{2,1,0:T(8,128)(2,1)}, u32[]{:S(2)}) %copy-start.2) | copy-done | bytes 524312
  5.3 0.0 copy-start.3
  5.3 1.0 %copy-done.3 = bf16[1,256,1024]{2,1,0:T(8,128)(2,1)S(1)} copy-done((bf16[1,256,1024]{2,1,0:T(8,128)(2,1)S(1)}, bf16[1,256,1024]{2,1,0:T(8,128)(2,1)}, u32[]{:S(2)}) %copy-start.3) | copy-done | bytes 524312
  6.3 0.0 copy-start.4
  6.3 0.8 %copy-done.4 = bf16[1,256,128]{2,1,0:T(8,128)(2,1)S(1)} copy-done((bf16[1,256,128]{2,1,0:T(8,128)(2,1)S(1)}, bf16[1,256,128]{2,1,0:T(8,128)(2,1)}, u32[]{:S(2)}) %copy-start.4) | copy-done | bytes 65560
  7.2 0.0 copy-start.5
  7.2 0.8 %copy-done.5 = bf16[1,256,128]{2,1,0:T(8,128)(2,1)S(1)} copy-done((bf16[1,256,128]{2,1,0:T(8,128)(2,1)S(1)}, bf16[1,256,128]{2,1,0:T(8,128)(2,1)}, u32[]{:S(2)}) %copy-start.5) | copy-done | bytes 65560
  8.0 0.0 copy-start.6
  8.0 0.7 %copy-done.6 = s32[1,256]{1,0:T(1,128)S(1)} copy-done((s32[1,256]{1,0:T(1,128)S(1)}, s32[1,256]{1,0:T(1,128)}, u32[]{:S(2)}) %copy-start.6) | copy-done | bytes 1048
  8.7 44.0 %shard_map.111 = (f32[1,256,1024]{2,1,0:T(8,128)S(1)}, f32[1,256,128]{2,1,0:T(8,128)S(1)}, f32[1,256,128]{2,1,0:T(8,128)S(1)}, f32[640,256]{1,0:T(8,128)S(1)}) custom-call(bf16[1,256,5120]{2,1,0:T(8,128)(2,1)S(1)} %copy-done, bf16[1,256,1024]{2,1,0:T(8,128)(2,1)S(1)} %copy-done.1, bf16[1,256,128]{2,1,0:T(8,128)(2,1)S(1)} %copy-done.4, ...), custom_call_target="tpu_custom_call" | custom-call | tf_op jit(solution)/shard_map/pallas_call | solution.py:352
  52.7 1.0 %copy.17 = f32[1,256,1024]{2,1,0:T(8,128)} copy(f32[1,256,1024]{2,1,0:T(8,128)S(1)} %get-tuple-element.8) | data formatting | bytes 2097152
  53.7 0.7 %copy.18 = f32[1,256,128]{2,1,0:T(8,128)} copy(f32[1,256,128]{2,1,0:T(8,128)S(1)} %get-tuple-element.9) | data formatting | bytes 262144
  54.3 0.7 %copy.19 = f32[1,256,128]{2,1,0:T(8,128)} copy(f32[1,256,128]{2,1,0:T(8,128)S(1)} %get-tuple-element.10) | data formatting | bytes 262144
  55.0 0.8 %copy.20 = f32[640,256]{1,0:T(8,128)} copy(f32[640,256]{1,0:T(8,128)S(1)} %get-tuple-element.11) | data formatting | bytes 1310720
Async XLA Ops:
  1.5 1.7 %copy-start = (bf16[1,256,5120]{2,1,0:T(8,128)(2,1)S(1)}, bf16[1,256,5120]{2,1,0:T(8,128)(2,1)}, u32[]{:S(2)}) copy-start(bf16[1,256,5120]{2,1,0:T(8,128)(2,1)} %x_ref.1) | copy-start | bytes 7864324
  3.2 1.0 %copy-start.1 = (bf16[1,256,1024]{2,1,0:T(8,128)(2,1)S(1)}, bf16[1,256,1024]{2,1,0:T(8,128)(2,1)}, u32[]{:S(2)}) copy-start(bf16[1,256,1024]{2,1,0:T(8,128)(2,1)} %q_ref.1) | copy-start | bytes 1572868
  4.2 1.0 %copy-start.2 = (bf16[1,256,1024]{2,1,0:T(8,128)(2,1)S(1)}, bf16[1,256,1024]{2,1,0:T(8,128)(2,1)}, u32[]{:S(2)}) copy-start(bf16[1,256,1024]{2,1,0:T(8,128)(2,1)} %o_ref.1) | copy-start | bytes 1572868
  5.3 1.0 %copy-start.3 = (bf16[1,256,1024]{2,1,0:T(8,128)(2,1)S(1)}, bf16[1,256,1024]{2,1,0:T(8,128)(2,1)}, u32[]{:S(2)}) copy-start(bf16[1,256,1024]{2,1,0:T(8,128)(2,1)} %g_ref.1) | copy-start | bytes 1572868
  6.3 0.8 %copy-start.4 = (bf16[1,256,128]{2,1,0:T(8,128)(2,1)S(1)}, bf16[1,256,128]{2,1,0:T(8,128)(2,1)}, u32[]{:S(2)}) copy-start(bf16[1,256,128]{2,1,0:T(8,128)(2,1)} %k_ref.1) | copy-start | bytes 196612
  7.2 0.8 %copy-start.5 = (bf16[1,256,128]{2,1,0:T(8,128)(2,1)S(1)}, bf16[1,256,128]{2,1,0:T(8,128)(2,1)}, u32[]{:S(2)}) copy-start(bf16[1,256,128]{2,1,0:T(8,128)(2,1)} %v_ref.1) | copy-start | bytes 196612
  8.0 0.7 %copy-start.6 = (s32[1,256]{1,0:T(1,128)S(1)}, s32[1,256]{1,0:T(1,128)}, u32[]{:S(2)}) copy-start(s32[1,256]{1,0:T(1,128)} %pos_ref.1) | copy-start | bytes 3076

commit v2 on v1

--- a/solution.py
+++ b/solution.py
@@ -1,4 +1,4 @@
-import functools
+import math
 
 import jax
 import jax.numpy as jnp
@@ -11,6 +11,8 @@
 MESH = pl.DeviceIdType.MESH
 NT = (((1,), (1,)), ((), ()))
 TN = (((0,), (0,)), ((), ()))
+LOG2E = math.log2(math.e)
+VMEM_BYTES = 60 * 1024 * 1024
 
 
 def passed_along(block, axis, distance):
@@ -117,9 +119,10 @@
 
 
 def fused_kernel(
-    x_ref, q_ref, k_ref, v_ref, o_ref, g_ref, lse_ref, pos_ref,
-    dq_ref, dk_ref, dv_ref, w_ref,
-    kv_peer, pos_send, pos_peer, stat, stat_t, part_own, part_send, part_recv, kv_all, x_all,
+    x_ref, q_hbm, k_hbm, v_hbm, o_hbm, g_hbm, lse_hbm, pos_hbm,
+    dq_hbm, dk_hbm, dv_hbm, w_hbm,
+    dq_ref, dk_ref, dv_ref, w_ref, save_sem,
+    q_ref, k_ref, v_ref, o_ref, g_ref, lse_ref, pos_ref, load_sem, kv_peer, pos_send, pos_peer, stat, stat_t, part_own, part_send, part_recv, kv_all, x_all,
     local_sem, kv_send, kv_recv, part_ssem, part_rsem,
     xd_send, xd_recv, xx_send, xx_recv, xc_send, xc_recv, g_send, g_recv,
 ):
@@ -148,6 +151,15 @@
             device_id=to, device_id_type=MESH,
         )
 
+    loads = [
+        pltpu.make_async_copy(src, dst, load_sem.at[i])
+        for i, (src, dst) in enumerate((
+            (pos_hbm, pos_ref), (k_hbm, k_ref), (v_hbm, v_ref), (lse_hbm, lse_ref),
+            (g_hbm, g_ref), (o_hbm, o_ref), (q_hbm, q_ref),
+        ))
+    ]
+    for copy in loads:
+        copy.start()
     barrier = pltpu.get_barrier_semaphore()
     for r in range(1, 8):
         pl.semaphore_signal(barrier, inc=1, device_id=ring(r)[1], device_id_type=MESH)
@@ -157,6 +169,8 @@
         x_ref.at[0, :, pl.ds(pl.multiple_of(me * width, 128), width)], x_all.at[0], local_sem
     )
     own_x.start()
+    for copy in loads[:3]:
+        copy.wait()
     pos_send[...] = jnp.broadcast_to(pos_ref[...], pos_send.shape)
     pl.semaphore_wait(barrier, 9)
 
@@ -168,7 +182,8 @@
     for copy in kv_copies:
         copy.start()
     direct = {}
-    for r in (4, 3, 5, 2, 6, 1, 7):
+
+    def send_x(r):
         other, to = ring(r)
         direct[r] = send(
             x_ref.at[0, rows_q, pl.ds(pl.multiple_of(other * width, 128), width)],
@@ -176,13 +191,18 @@
         )
         direct[r].start()
 
+    for r in (4, 2, 6):
+        send_x(r)
+
+    for copy in loads[3:]:
+        copy.wait()
     stat[...] = jnp.zeros_like(stat)
-    stat[:, 0:heads] = lse_ref[0]
     for i in range(heads):
         cols = slice(i * HD, (i + 1) * HD)
         prod = g_ref[0, :, cols].astype(jnp.float32) * o_ref[0, :, cols].astype(jnp.float32)
-        stat[:, heads + i:heads + i + 1] = jnp.sum(prod, axis=1, keepdims=True)
+        stat[:, i:i + 1] = jnp.sum(prod, axis=1, keepdims=True)
     stat_t[...] = jnp.transpose(stat[...])
+    lse_low = lse_ref[0] * LOG2E
     pos_row = pos_ref[...].astype(jnp.float32)
 
     def column(row):
@@ -191,16 +211,16 @@
     def chunk(key, value, key_pos, first, last):
         visible = key_pos <= pos_row
 
-        def one_head(i, carry):
-            dk, dv = carry
-            cols = pl.ds(pl.multiple_of(i * HD, HD), HD)
+        dk = jnp.zeros((half, HD), jnp.float32)
+        dv = jnp.zeros((half, HD), jnp.float32)
+        for i in range(heads):
+            cols = slice(i * HD, (i + 1) * HD)
             query, grad = q_ref[0, :, cols], g_ref[0, :, cols]
-            lse_row = stat_t[pl.ds(i, 1), :]
-            delta_row = stat_t[pl.ds(i + heads, 1), :]
-            scores = lax.dot_general(key, query, NT, preferred_element_type=jnp.float32) * factor
-            probs = jnp.where(visible, jnp.exp(scores - lse_row), jnp.float32(0.0))
+            scores = lax.dot_general(key, query, NT, preferred_element_type=jnp.float32)
+            probs = jnp.exp2(scores * (factor * LOG2E) - lse_low[i:i + 1, :])
+            probs = jnp.where(visible, probs, jnp.float32(0.0))
             dprobs = lax.dot_general(value, grad, NT, preferred_element_type=jnp.float32)
-            dscores = (probs * (dprobs - delta_row)).astype(jnp.bfloat16)
+            dscores = (probs * (dprobs - stat_t[i:i + 1, :])).astype(jnp.bfloat16)
             dv = dv + jnp.dot(probs.astype(jnp.bfloat16), grad, preferred_element_type=jnp.float32)
             dk = dk + jnp.dot(dscores, query, preferred_element_type=jnp.float32)
             dq = lax.dot_general(dscores, key, TN, preferred_element_type=jnp.float32)
@@ -209,10 +229,6 @@
             if last:
                 dq = dq * factor
             dq_ref[0, :, cols] = dq
-            return dk, dv
-
-        zero = jnp.zeros((half, HD), jnp.float32)
-        dk, dv = lax.fori_loop(0, heads, one_head, (zero, zero), unroll=2)
         return dk * factor, dv
 
     def own_chunk(c, first, last):
@@ -221,8 +237,26 @@
         part_own[c, :, 0:HD] = dk
         part_own[c, :, HD:] = dv
 
+    over_x, over_core = {}, {}
+
+    def forward_x(r):
+        direct[r].wait_recv()
+        over_x[r] = send(
+            x_all.at[r, rows_q, :], x_all.at[r, rows_q, :], xx_send.at[r], xx_recv.at[r], x_peer
+        )
+        over_x[r].start()
+
+    def forward_core(r):
+        over_x[r].wait_recv()
+        over_core[r] = send(
+            x_all.at[r, rows_h, :], x_all.at[r, rows_h, :], xc_send.at[r], xc_recv.at[r], core_peer
+        )
+        over_core[r].start()
+
     own_col = column(pos_row)
     own_chunk(0, True, False)
+    for r in (3, 5, 1, 7):
+        send_x(r)
 
     for copy in kv_copies:
         copy.wait_recv()
@@ -238,7 +272,16 @@
         )
         copy.start()
         part_copies.append(copy)
+    for r in (2, 6, 4):
+        forward_x(r)
     own_chunk(1, False, True)
+    saves = [
+        pltpu.make_async_copy(src, dst, save_sem.at[i])
+        for i, (src, dst) in enumerate((
+            (dq_ref, dq_hbm), (dk_ref, dk_hbm), (dv_ref, dv_hbm), (w_ref, w_hbm),
+        ))
+    ]
+    saves[0].start()
 
     up, down = {"dp": z + 1}, {"dp": z - 1}
     first_z, last_z = 1 - (z + 3) // 4, z // 3
@@ -291,46 +334,33 @@
                 )
             )
 
-    over_x, over_core = {}, {}
-
-    def forward_x(r):
-        direct[r].wait_recv()
-        over_x[r] = send(
-            x_all.at[r, rows_q, :], x_all.at[r, rows_q, :], xx_send.at[r], xx_recv.at[r], x_peer
-        )
-        over_x[r].start()
-
-    def forward_core(r):
-        over_x[r].wait_recv()
-        over_core[r] = send(
-            x_all.at[r, rows_h, :], x_all.at[r, rows_h, :], xc_send.at[r], xc_recv.at[r], core_peer
-        )
-        over_core[r].start()
-
     def add(r, first=False):
         term = lax.dot_general(x_all[r], kv_all[r], TN, preferred_element_type=jnp.float32)
         w_ref[...] = term if first else w_ref[...] + term
 
-    for r in (1, 7, 2, 6):
-        forward_x(r)
+    saves[1].start()
+    saves[2].start()
+    own_x.wait()
+    add(0, True)
     forward_kv(1)
-    for r in (3, 5, 4):
+    for r in (2, 6, 4):
+        forward_core(r)
+    for r in (1, 7, 3, 5):
         forward_x(r)
     forward_kv(2)
-    for r in (1, 7, 2, 6, 3, 5, 4):
-        forward_core(r)
     forward_kv(3)
-    own_x.wait()
-    add(0, True)
     for r in (2, 6, 4):
         over_core[r].wait_recv()
         add(r)
+    for r in (1, 7, 3, 5):
+        forward_core(r)
     for r in (1, 7, 3, 5):
         over_core[r].wait_recv()
         arrived(0, r)
         arrived(1, r)
         add(r)
 
+    saves[3].start()
     for copy in kv_copies + part_copies:
         copy.wait_send()
     for r in range(1, 8):
@@ -341,25 +371,45 @@
         copies[0].wait_send()
         pl.when(to_up)(copies[1].wait_send)
         pl.when(to_down)(copies[2].wait_send)
+    for copy in saves:
+        copy.wait()
+
+
+def write_kernel(*refs):
+    sources, results, sem = refs[:4], refs[4:8], refs[8]
+    copies = [
+        pltpu.make_async_copy(src, dst, sem.at[i])
+        for i, (src, dst) in enumerate(zip(sources, results))
+    ]
+    for copy in copies:
+        copy.start()
+    for copy in copies:
+        copy.wait()
 
 
 def fused(inputs, queries, keys, values, outputs, out_grad, lse, positions):
     tokens = queries.shape[1]
     width = inputs.shape[2] // 8
-    vmem = pl.BlockSpec(memory_space=pltpu.VMEM)
+    hbm = pl.BlockSpec(memory_space=pltpu.HBM)
     dma = pltpu.SemaphoreType.DMA
     f32, bf16 = jnp.float32, jnp.bfloat16
-    return pl.pallas_call(
+    lse_rows = jnp.transpose(lse, (0, 2, 1))
+    args = (inputs, queries, keys, values, outputs, out_grad, lse_rows, positions)
+    shapes = (
+        jax.ShapeDtypeStruct(queries.shape, f32),
+        jax.ShapeDtypeStruct(keys.shape, f32),
+        jax.ShapeDtypeStruct(values.shape, f32),
+        jax.ShapeDtypeStruct((width, 2 * HD), f32),
+    )
+    grads = pl.pallas_call(
         fused_kernel,
-        out_shape=(
-            jax.ShapeDtypeStruct(queries.shape, f32),
-            jax.ShapeDtypeStruct(keys.shape, f32),
-            jax.ShapeDtypeStruct(values.shape, f32),
-            jax.ShapeDtypeStruct((width, 2 * HD), f32),
-        ),
-        in_specs=[pl.BlockSpec(memory_space=pl.ANY)] + [vmem] * 7,
-        out_specs=(vmem,) * 4,
-        scratch_shapes=[
+        out_shape=shapes,
+        in_specs=[hbm] * 8,
+        out_specs=(hbm,) * 4,
+        scratch_shapes=[pltpu.VMEM(a.shape, a.dtype) for a in shapes] + [
+            dma((4,)),
+        ] + [pltpu.VMEM(a.shape, a.dtype) for a in args[1:]] + [
+            dma((7,)),
             pltpu.VMEM((2, tokens, HD), bf16),
             pltpu.VMEM((8, tokens), jnp.int32),
             pltpu.VMEM((8, tokens), jnp.int32),
@@ -379,9 +429,17 @@
             dma((2, 4, 3)), dma((2, 8)),
         ],
         compiler_params=pltpu.CompilerParams(
-            collective_id=0, has_side_effects=True, vmem_limit_bytes=40 * 1024 * 1024
+            collective_id=0, has_side_effects=True, vmem_limit_bytes=VMEM_BYTES
         ),
-    )(inputs, queries, keys, values, outputs, out_grad, lse, positions)
+    )(*args)
+    return pl.pallas_call(
+        write_kernel,
+        out_shape=shapes,
+        in_specs=[hbm] * 4,
+        out_specs=(hbm,) * 4,
+        scratch_shapes=[dma((4,))],
+        compiler_params=pltpu.CompilerParams(vmem_limit_bytes=VMEM_BYTES),
+    )(*grads)
 
 
 def fits(mesh):

time: 56.3 us -> 99.5 us (1.77)
  Pallas kernels: 44 us -> 98.7 us
  local copies, waits for them, and re-layouts: 11.2 us -> 0 us
    pallas_call x1 -> x2, Pallas kernels: 44 us -> 98.7 us  [the longest x1 60.7 us: fused(): pl.pallas_call(write_kernel, out_shape=shapes, in_specs=[hbm] * 4, out_sp...]
    unnamed x19 -> x0, local copies, waits for them, and re-layouts: 11.2 us -> none
where the time goes in v2:
time: 99.5 us; the launch traced here: 99.4 us
  Pallas kernels  98.7 us (99%)
    pallas_call x1, Pallas kernels, fused(): pl.pallas_call(write_kernel, out_shape=shapes, in_specs=[hbm] * 4, out_sp...  60.7 us
    pallas_call x1, Pallas kernels, fused(): pl.pallas_call(fused_kernel, out_shape=shapes, in_specs=[hbm] * 8, out_sp...  38 us

profile of v2, /device:TPU:0, one launch (start us, length us, event | category | flops | bytes accessed | tf_op | source)
XLA Modules:
  0.0 99.4 jit_solution(12661106321019097599)
XLA Ops:
  0.6 38.0 %shard_map.111 = (f32[1,256,1024]{2,1,0:T(8,128)}, f32[1,256,128]{2,1,0:T(8,128)}, f32[1,256,128]{2,1,0:T(8,128)}, f32[640,256]{1,0:T(8,128)}) custom-call(bf16[1,256,5120]{2,1,0:T(8,128)(2,1)} %x_ref.1, bf16[1,256,1024]{2,1,0:T(8,128)(2,1)} %q_hbm.1, bf16[1,256,128]{2,1,0:T(8,128)(2,1)} %k_hbm.1, bf16[1,256,128]{2,1,0:T(8,128)(2,1)} %v_hbm.1, ...), custom_call_target="tpu_custom_call" | custom-call | tf_op jit(solution)/shard_map/pallas_call | solution.py:404
  38.7 60.7 %shard_map.112 = (f32[1,256,1024]{2,1,0:T(8,128)}, f32[1,256,128]{2,1,0:T(8,128)}, f32[1,256,128]{2,1,0:T(8,128)}, f32[640,256]{1,0:T(8,128)}) custom-call(f32[1,256,1024]{2,1,0:T(8,128)} %get-tuple-element.8.refs_0_, f32[1,256,128]{2,1,0:T(8,128)} %get-tuple-element.9.refs_1_, f32[1,256,128]{2,1,0:T(8,128)} %get-tuple-element.10.refs_2_, ...), custom_call_target="tpu_custom_call" | custom-call | tf_op jit(solution)/shard_map/pallas_call | solution.py:435

commit v3 on v2

--- a/solution.py
+++ b/solution.py
@@ -122,7 +122,8 @@
     x_ref, q_hbm, k_hbm, v_hbm, o_hbm, g_hbm, lse_hbm, pos_hbm,
     dq_hbm, dk_hbm, dv_hbm, w_hbm,
     dq_ref, dk_ref, dv_ref, w_ref, save_sem,
-    q_ref, k_ref, v_ref, o_ref, g_ref, lse_ref, pos_ref, load_sem, kv_peer, pos_send, pos_peer, stat, stat_t, part_own, part_send, part_recv, kv_all, x_all,
+    q_ref, k_ref, v_ref, o_ref, g_ref, lse_ref, pos_ref, load_sem,
+    kv_peer, pos_send, pos_peer, qt_ref, gt_ref, dqt_ref, xt_all, part_send, part_recv, kv_all, x_all,
     local_sem, kv_send, kv_recv, part_ssem, part_rsem,
     xd_send, xd_recv, xx_send, xx_recv, xc_send, xc_recv, g_send, g_recv,
 ):
@@ -196,46 +197,45 @@
 
     for copy in loads[3:]:
         copy.wait()
-    stat[...] = jnp.zeros_like(stat)
+    ones = jnp.ones((8, HD), jnp.bfloat16)
+    delta = []
     for i in range(heads):
         cols = slice(i * HD, (i + 1) * HD)
+        qt_ref[i] = jnp.transpose(q_ref[0, :, cols])
+        gt_ref[i] = jnp.transpose(g_ref[0, :, cols])
         prod = g_ref[0, :, cols].astype(jnp.float32) * o_ref[0, :, cols].astype(jnp.float32)
-        stat[:, i:i + 1] = jnp.sum(prod, axis=1, keepdims=True)
-    stat_t[...] = jnp.transpose(stat[...])
+        high = prod.astype(jnp.bfloat16)
+        low = (prod - high.astype(jnp.float32)).astype(jnp.bfloat16)
+        both = lax.dot_general(ones, high, NT, preferred_element_type=jnp.float32)
+        both = both + lax.dot_general(ones, low, NT, preferred_element_type=jnp.float32)
+        delta.append(both[0:1, :])
     lse_low = lse_ref[0] * LOG2E
     pos_row = pos_ref[...].astype(jnp.float32)
 
     def column(row):
         return jnp.transpose(jnp.broadcast_to(row, (HD, tokens)))
 
-    def chunk(key, value, key_pos, first, last):
+    def block(key, value, key_pos, first):
         visible = key_pos <= pos_row
-
-        dk = jnp.zeros((half, HD), jnp.float32)
-        dv = jnp.zeros((half, HD), jnp.float32)
+        key_t = jnp.transpose(key)
+        dk = jnp.zeros((tokens, HD), jnp.float32)
+        dv = jnp.zeros((tokens, HD), jnp.float32)
         for i in range(heads):
             cols = slice(i * HD, (i + 1) * HD)
-            query, grad = q_ref[0, :, cols], g_ref[0, :, cols]
-            scores = lax.dot_general(key, query, NT, preferred_element_type=jnp.float32)
+            scores = jnp.dot(key, qt_ref[i], preferred_element_type=jnp.float32)
             probs = jnp.exp2(scores * (factor * LOG2E) - lse_low[i:i + 1, :])
             probs = jnp.where(visible, probs, jnp.float32(0.0))
-            dprobs = lax.dot_general(value, grad, NT, preferred_element_type=jnp.float32)
-            dscores = (probs * (dprobs - stat_t[i:i + 1, :])).astype(jnp.bfloat16)
-            dv = dv + jnp.dot(probs.astype(jnp.bfloat16), grad, preferred_element_type=jnp.float32)
-            dk = dk + jnp.dot(dscores, query, preferred_element_type=jnp.float32)
-            dq = lax.dot_general(dscores, key, TN, preferred_element_type=jnp.float32)
-            if not first:
-                dq = dq_ref[0, :, cols] + dq
-            if last:
-                dq = dq * factor
-            dq_ref[0, :, cols] = dq
+            dprobs = jnp.dot(value, gt_ref[i], preferred_element_type=jnp.float32)
+            dscores = (probs * (dprobs - delta[i])).astype(jnp.bfloat16)
+            probs = probs.astype(jnp.bfloat16)
+            dv = dv + jnp.dot(probs, g_ref[0, :, cols], preferred_element_type=jnp.float32)
+            dk = dk + jnp.dot(dscores, q_ref[0, :, cols], preferred_element_type=jnp.float32)
+            dqt = jnp.dot(key_t, dscores, preferred_element_type=jnp.float32)
+            if first:
+                dqt_ref[i] = dqt
+            else:
+                dq_ref[0, :, cols] = jnp.transpose((dqt_ref[i] + dqt) * factor)
         return dk * factor, dv
-
-    def own_chunk(c, first, last):
-        rows = slice(c * half, (c + 1) * half)
-        dk, dv = chunk(k_ref[0, rows, :], v_ref[0, rows, :], own_col[rows, 0:1], first, last)
-        part_own[c, :, 0:HD] = dk
-        part_own[c, :, HD:] = dv
 
     over_x, over_core = {}, {}
 
@@ -253,20 +253,18 @@
         )
         over_core[r].start()
 
-    own_col = column(pos_row)
-    own_chunk(0, True, False)
+    for copy in kv_copies:
+        copy.wait_recv()
     for r in (3, 5, 1, 7):
         send_x(r)
-
-    for copy in kv_copies:
-        copy.wait_recv()
-    peer_col = column(pos_peer[0:1, :].astype(jnp.float32))
+    dk, dv = block(
+        kv_peer[0], kv_peer[1], column(pos_peer[0:1, :].astype(jnp.float32))[:, 0:1], True
+    )
     part_copies = []
     for c in range(2):
         rows = slice(c * half, (c + 1) * half)
-        dk, dv = chunk(kv_peer[0, rows, :], kv_peer[1, rows, :], peer_col[rows, 0:1], False, False)
-        part_send[c, :, 0:HD] = dk.astype(jnp.bfloat16)
-        part_send[c, :, HD:] = dv.astype(jnp.bfloat16)
+        part_send[c, :, 0:HD] = dk[rows].astype(jnp.bfloat16)
+        part_send[c, :, HD:] = dv[rows].astype(jnp.bfloat16)
         copy = send(
             part_send.at[c], part_recv.at[c], part_ssem.at[c], part_rsem.at[c], y_peer
         )
@@ -274,7 +272,7 @@
         part_copies.append(copy)
     for r in (2, 6, 4):
         forward_x(r)
-    own_chunk(1, False, True)
+    dk_own, dv_own = block(k_ref[0], v_ref[0], column(pos_row)[:, 0:1], False)
     saves = [
         pltpu.make_async_copy(src, dst, save_sem.at[i])
         for i, (src, dst) in enumerate((
@@ -304,10 +302,12 @@
     for c in range(2):
         rows = slice(c * half, (c + 1) * half)
         part_copies[c].wait_recv()
-        total = part_own[c] + part_recv[c].astype(jnp.float32)
-        dk_ref[0, rows, :] = total[:, 0:HD]
-        dv_ref[0, rows, :] = total[:, HD:]
-        kv_all[0, rows, :] = total.astype(jnp.bfloat16)
+        dk = dk_own[rows] + part_recv[c, :, 0:HD].astype(jnp.float32)
+        dv = dv_own[rows] + part_recv[c, :, HD:].astype(jnp.float32)
+        dk_ref[0, rows, :] = dk
+        dv_ref[0, rows, :] = dv
+        kv_all[0, rows, 0:HD] = dk.astype(jnp.bfloat16)
+        kv_all[0, rows, HD:] = dv.astype(jnp.bfloat16)
         passed.append(pass_block(c, 0, 0, z < 3, z > 0))
 
     def arrived(c, r):
@@ -316,13 +316,13 @@
             kv_all.at[r, rows, :], kv_all.at[r, rows, :], g_send.at[c, 0, 0], g_recv.at[c, r], y_peer
         ).wait_recv()
 
+    turns = (
+        2 + 4 * first_z, 6 - 2 * (first_z + last_z), 4 - 2 * first_z + 2 * last_z
+    )
+    odd_turns = [(r + 7 + 2 * y) % 8 for r in (0,) + turns]
+
     def forward_kv(step):
-        if step == 1:
-            r = 2 + 4 * first_z
-        elif step == 2:
-            r = 6 - 2 * (first_z + last_z)
-        else:
-            r = 4 - 2 * first_z + 2 * last_z
+        r = turns[step - 1]
         rising = z >= r // 2
         for c in range(2):
             arrived(c, r)
@@ -334,32 +334,40 @@
                 )
             )
 
+    def turn_x(r):
+        xt_all[r] = jnp.transpose(x_all[r])
+
     def add(r, first=False):
-        term = lax.dot_general(x_all[r], kv_all[r], TN, preferred_element_type=jnp.float32)
+        term = jnp.dot(xt_all[r], kv_all[r], preferred_element_type=jnp.float32)
         w_ref[...] = term if first else w_ref[...] + term
 
     saves[1].start()
     saves[2].start()
+    for r in (2, 6, 4):
+        forward_core(r)
     own_x.wait()
+    turn_x(0)
     add(0, True)
     forward_kv(1)
-    for r in (2, 6, 4):
-        forward_core(r)
     for r in (1, 7, 3, 5):
         forward_x(r)
-    forward_kv(2)
-    forward_kv(3)
     for r in (2, 6, 4):
         over_core[r].wait_recv()
-        add(r)
+        turn_x(r)
+    forward_kv(2)
+    add(turns[0])
+    add(turns[1])
+    forward_kv(3)
     for r in (1, 7, 3, 5):
         forward_core(r)
+    add(turns[2])
     for r in (1, 7, 3, 5):
         over_core[r].wait_recv()
+        turn_x(r)
+    for r in odd_turns:
         arrived(0, r)
         arrived(1, r)
         add(r)
-
     saves[3].start()
     for copy in kv_copies + part_copies:
         copy.wait_send()
@@ -376,15 +384,24 @@
 
 
 def write_kernel(*refs):
-    sources, results, sem = refs[:4], refs[4:8], refs[8]
-    copies = [
-        pltpu.make_async_copy(src, dst, sem.at[i])
-        for i, (src, dst) in enumerate(zip(sources, results))
-    ]
-    for copy in copies:
-        copy.start()
-    for copy in copies:
-        copy.wait()
+    sources, results, held, sem_in, sem_out = refs[:4], refs[4:8], refs[8:12], refs[12], refs[13]
+    whole = [(i, slice(None)) for i in range(1, 4)]
+    quarter = held[0].shape[1] // 4
+    parts = whole + [(0, slice(c * quarter, (c + 1) * quarter)) for c in range(4)]
+    copies = []
+    for n, (i, rows) in enumerate(parts):
+        at = (0, rows) if i == 0 else (slice(None),)
+        copies.append((
+            pltpu.make_async_copy(sources[i].at[at], held[i].at[at], sem_in.at[n]),
+            pltpu.make_async_copy(held[i].at[at], results[i].at[at], sem_out.at[n]),
+        ))
+    for into, _ in copies:
+        into.start()
+    for into, out in copies:
+        into.wait()
+        out.start()
+    for _, out in copies:
+        out.wait()
 
 
 def fused(inputs, queries, keys, values, outputs, out_grad, lse, positions):
@@ -413,9 +430,10 @@
             pltpu.VMEM((2, tokens, HD), bf16),
             pltpu.VMEM((8, tokens), jnp.int32),
             pltpu.VMEM((8, tokens), jnp.int32),
-            pltpu.VMEM((tokens, HD), f32),
-            pltpu.VMEM((HD, tokens), f32),
-            pltpu.VMEM((2, tokens // 2, 2 * HD), f32),
+            pltpu.VMEM((queries.shape[2] // HD, HD, tokens), bf16),
+            pltpu.VMEM((queries.shape[2] // HD, HD, tokens), bf16),
+            pltpu.VMEM((queries.shape[2] // HD, HD, tokens), f32),
+            pltpu.VMEM((8, width, tokens), bf16),
             pltpu.VMEM((2, tokens // 2, 2 * HD), bf16),
             pltpu.VMEM((2, tokens // 2, 2 * HD), bf16),
             pltpu.VMEM((8, tokens, 2 * HD), bf16),
@@ -437,7 +455,7 @@
         out_shape=shapes,
         in_specs=[hbm] * 4,
         out_specs=(hbm,) * 4,
-        scratch_shapes=[dma((4,))],
+        scratch_shapes=[pltpu.VMEM(a.shape, a.dtype) for a in shapes] + [dma((7,)), dma((7,))],
         compiler_params=pltpu.CompilerParams(vmem_limit_bytes=VMEM_BYTES),
     )(*grads)
 

time: 99.5 us -> 42.4 us (0.43)
  Pallas kernels: 98.7 us -> 41.6 us
    pallas_call x1, Pallas kernels: 60.7 us -> 2.53 us  [fused(): pl.pallas_call(write_kernel, out_shape=shapes, in_specs=[hbm] * 4, out_sp...]
    pallas_call x1, Pallas kernels: 38 us -> 39.1 us  [fused(): pl.pallas_call(fused_kernel, out_shape=shapes, in_specs=[hbm] * 8, out_sp...]
where the time goes in v3:
time: 42.4 us; the launch traced here: 42.2 us
  Pallas kernels  41.6 us (98%)
  between operations  0.64 us (2%)
    pallas_call x1, Pallas kernels, fused(): pl.pallas_call(fused_kernel, out_shape=shapes, in_specs=[hbm] * 8, out_sp...  39.1 us
    pallas_call x1, Pallas kernels, fused(): pl.pallas_call(write_kernel, out_shape=shapes, in_specs=[hbm] * 4, out_sp...  2.53 us

profile of v3, /device:TPU:0, one launch (start us, length us, event | category | flops | bytes accessed | tf_op | source)
XLA Modules:
  0.0 42.2 jit_solution(17639752925784816000)
XLA Ops:
  0.6 39.1 %shard_map.111 = (f32[1,256,1024]{2,1,0:T(8,128)}, f32[1,256,128]{2,1,0:T(8,128)}, f32[1,256,128]{2,1,0:T(8,128)}, f32[640,256]{1,0:T(8,128)}) custom-call(bf16[1,256,5120]{2,1,0:T(8,128)(2,1)} %x_ref.1, bf16[1,256,1024]{2,1,0:T(8,128)(2,1)} %q_hbm.1, bf16[1,256,128]{2,1,0:T(8,128)(2,1)} %k_hbm.1, bf16[1,256,128]{2,1,0:T(8,128)(2,1)} %v_hbm.1, ...), custom_call_target="tpu_custom_call" | custom-call | tf_op jit(solution)/shard_map/pallas_call | solution.py:421
  39.7 2.5 %shard_map.112 = (f32[1,256,1024]{2,1,0:T(8,128)}, f32[1,256,128]{2,1,0:T(8,128)}, f32[1,256,128]{2,1,0:T(8,128)}, f32[640,256]{1,0:T(8,128)}) custom-call(f32[1,256,1024]{2,1,0:T(8,128)} %get-tuple-element.8.refs_0_, f32[1,256,128]{2,1,0:T(8,128)} %get-tuple-element.9.refs_1_, f32[1,256,128]{2,1,0:T(8,128)} %get-tuple-element.10.refs_2_, ...), custom_call_target="tpu_custom_call" | custom-call | tf_op jit(solution)/shard_map/pallas_call | solution.py:453

commit v4 on v3

--- a/solution.py
+++ b/solution.py
@@ -182,18 +182,20 @@
     ]
     for copy in kv_copies:
         copy.start()
-    direct = {}
-
-    def send_x(r):
-        other, to = ring(r)
-        direct[r] = send(
+    first_z, last_z = 1 - (z + 3) // 4, z // 3
+    turns = (2 + 4 * first_z, 6 - 2 * (first_z + last_z), 4 - 2 * first_z + 2 * last_z)
+    odd_turns = [(r + 7 + 2 * y) % 8 for r in (0,) + turns]
+    order = [r for pair in zip(odd_turns, turns) for r in pair] + odd_turns[3:]
+
+    def direct(r, other, to):
+        return send(
             x_ref.at[0, rows_q, pl.ds(pl.multiple_of(other * width, 128), width)],
             x_all.at[r, rows_q, :], xd_send.at[r], xd_recv.at[r], to,
         )
-        direct[r].start()
-
-    for r in (4, 2, 6):
-        send_x(r)
+
+    for r in order:
+        back = (8 - r) % 8
+        direct(back, *ring(back)).start()
 
     for copy in loads[3:]:
         copy.wait()
@@ -215,7 +217,7 @@
     def column(row):
         return jnp.transpose(jnp.broadcast_to(row, (HD, tokens)))
 
-    def block(key, value, key_pos, first):
+    def block(key, value, key_pos, first, forwards):
         visible = key_pos <= pos_row
         key_t = jnp.transpose(key)
         dk = jnp.zeros((tokens, HD), jnp.float32)
@@ -235,30 +237,30 @@
                 dqt_ref[i] = dqt
             else:
                 dq_ref[0, :, cols] = jnp.transpose((dqt_ref[i] + dqt) * factor)
+            if i in forwards:
+                forward_x(forwards[i])
         return dk * factor, dv
 
-    over_x, over_core = {}, {}
-
-    def forward_x(r):
-        direct[r].wait_recv()
-        over_x[r] = send(
-            x_all.at[r, rows_q, :], x_all.at[r, rows_q, :], xx_send.at[r], xx_recv.at[r], x_peer
-        )
-        over_x[r].start()
-
-    def forward_core(r):
-        over_x[r].wait_recv()
-        over_core[r] = send(
-            x_all.at[r, rows_h, :], x_all.at[r, rows_h, :], xc_send.at[r], xc_recv.at[r], core_peer
-        )
-        over_core[r].start()
+    def over_x(r):
+        part = x_all.at[r, rows_q, :]
+        return send(part, part, xx_send.at[r], xx_recv.at[r], x_peer)
+
+    def over_core(r):
+        part = x_all.at[r, rows_h, :]
+        return send(part, part, xc_send.at[r], xc_recv.at[r], core_peer)
+
+    def forward_x(n):
+        direct(order[n], *ring(order[n])).wait_recv()
+        over_x(order[n]).start()
+
+    def forward_core(n):
+        over_x(order[n]).wait_recv()
+        over_core(order[n]).start()
 
     for copy in kv_copies:
         copy.wait_recv()
-    for r in (3, 5, 1, 7):
-        send_x(r)
     dk, dv = block(
-        kv_peer[0], kv_peer[1], column(pos_peer[0:1, :].astype(jnp.float32))[:, 0:1], True
+        kv_peer[0], kv_peer[1], column(pos_peer[0:1, :].astype(jnp.float32))[:, 0:1], True, {}
     )
     part_copies = []
     for c in range(2):
@@ -270,9 +272,9 @@
         )
         copy.start()
         part_copies.append(copy)
-    for r in (2, 6, 4):
-        forward_x(r)
-    dk_own, dv_own = block(k_ref[0], v_ref[0], column(pos_row)[:, 0:1], False)
+    dk_own, dv_own = block(
+        k_ref[0], v_ref[0], column(pos_row)[:, 0:1], False, {0: 0, 2: 1, 4: 2, 6: 3}
+    )
     saves = [
         pltpu.make_async_copy(src, dst, save_sem.at[i])
         for i, (src, dst) in enumerate((
@@ -282,7 +284,6 @@
     saves[0].start()
 
     up, down = {"dp": z + 1}, {"dp": z - 1}
-    first_z, last_z = 1 - (z + 3) // 4, z // 3
 
     def pass_block(c, step, r, to_up, to_down):
         rows = slice(c * half, (c + 1) * half)
@@ -316,11 +317,6 @@
             kv_all.at[r, rows, :], kv_all.at[r, rows, :], g_send.at[c, 0, 0], g_recv.at[c, r], y_peer
         ).wait_recv()
 
-    turns = (
-        2 + 4 * first_z, 6 - 2 * (first_z + last_z), 4 - 2 * first_z + 2 * last_z
-    )
-    odd_turns = [(r + 7 + 2 * y) % 8 for r in (0,) + turns]
-
     def forward_kv(step):
         r = turns[step - 1]
         rising = z >= r // 2
@@ -334,47 +330,56 @@
                 )
             )
 
-    def turn_x(r):
-        xt_all[r] = jnp.transpose(x_all[r])
-
-    def add(r, first=False):
-        term = jnp.dot(xt_all[r], kv_all[r], preferred_element_type=jnp.float32)
-        w_ref[...] = term if first else w_ref[...] + term
+    def turn_x(n):
+        over_core(order[n]).wait_recv()
+        xt_all[order[n]] = jnp.transpose(x_all[order[n]])
+
+    def add(r):
+        w_ref[...] += jnp.dot(xt_all[r], kv_all[r], preferred_element_type=jnp.float32)
+
+    def add_odd(n):
+        arrived(0, odd_turns[n])
+        arrived(1, odd_turns[n])
+        add(odd_turns[n])
 
     saves[1].start()
     saves[2].start()
-    for r in (2, 6, 4):
-        forward_core(r)
+    forward_x(4)
+    for n in (0, 1, 2):
+        forward_core(n)
     own_x.wait()
-    turn_x(0)
-    add(0, True)
+    xt_all[0] = jnp.transpose(x_all[0])
+    w_ref[...] = jnp.dot(xt_all[0], kv_all[0], preferred_element_type=jnp.float32)
     forward_kv(1)
-    for r in (1, 7, 3, 5):
-        forward_x(r)
-    for r in (2, 6, 4):
-        over_core[r].wait_recv()
-        turn_x(r)
+    forward_x(5)
+    forward_x(6)
+    forward_core(3)
+    forward_core(4)
+    for n in (0, 1, 2):
+        turn_x(n)
     forward_kv(2)
     add(turns[0])
+    add_odd(0)
+    turn_x(3)
+    forward_core(5)
     add(turns[1])
+    turn_x(4)
     forward_kv(3)
-    for r in (1, 7, 3, 5):
-        forward_core(r)
+    forward_core(6)
+    add_odd(1)
+    turn_x(5)
     add(turns[2])
-    for r in (1, 7, 3, 5):
-        over_core[r].wait_recv()
-        turn_x(r)
-    for r in odd_turns:
-        arrived(0, r)
-        arrived(1, r)
-        add(r)
+    add_odd(2)
+    turn_x(6)
+    add_odd(3)
+
     saves[3].start()
     for copy in kv_copies + part_copies:
         copy.wait_send()
     for r in range(1, 8):
-        direct[r].wait_send()
-        over_x[r].wait_send()
-        over_core[r].wait_send()
+        direct(r, *ring(r)).wait_send()
+        over_x(r).wait_send()
+        over_core(r).wait_send()
     for copies, to_up, to_down in passed:
         copies[0].wait_send()
         pl.when(to_up)(copies[1].wait_send)

time: 42.4 us -> 44.5 us (1.050)
  Pallas kernels: 41.6 us -> 43.7 us
    pallas_call x1, Pallas kernels: 39.1 us -> 41.2 us  [fused(): pl.pallas_call(fused_kernel, out_shape=shapes, in_specs=[hbm] * 8, out_sp...]
where the time goes in v4:
time: 44.5 us; the launch traced here: 44.3 us
  Pallas kernels  43.7 us (98%)
  between operations  0.64 us (1%)
    pallas_call x1, Pallas kernels, fused(): pl.pallas_call(fused_kernel, out_shape=shapes, in_specs=[hbm] * 8, out_sp...  41.2 us
    pallas_call x1, Pallas kernels, fused(): pl.pallas_call(write_kernel, out_shape=shapes, in_specs=[hbm] * 4, out_sp...  2.53 us

profile of v4, /device:TPU:0, one launch (start us, length us, event | category | flops | bytes accessed | tf_op | source)
XLA Modules:
  0.0 44.3 jit_solution(4145400018641850414)
XLA Ops:
  0.6 41.2 %shard_map.111 = (f32[1,256,1024]{2,1,0:T(8,128)}, f32[1,256,128]{2,1,0:T(8,128)}, f32[1,256,128]{2,1,0:T(8,128)}, f32[640,256]{1,0:T(8,128)}) custom-call(bf16[1,256,5120]{2,1,0:T(8,128)(2,1)} %x_ref.1, bf16[1,256,1024]{2,1,0:T(8,128)(2,1)} %q_hbm.1, bf16[1,256,128]{2,1,0:T(8,128)(2,1)} %k_hbm.1, bf16[1,256,128]{2,1,0:T(8,128)(2,1)} %v_hbm.1, ...), custom_call_target="tpu_custom_call" | custom-call | tf_op jit(solution)/shard_map/pallas_call | solution.py:426
  41.8 2.5 %shard_map.112 = (f32[1,256,1024]{2,1,0:T(8,128)}, f32[1,256,128]{2,1,0:T(8,128)}, f32[1,256,128]{2,1,0:T(8,128)}, f32[640,256]{1,0:T(8,128)}) custom-call(f32[1,256,1024]{2,1,0:T(8,128)} %get-tuple-element.8.refs_0_, f32[1,256,128]{2,1,0:T(8,128)} %get-tuple-element.9.refs_1_, f32[1,256,128]{2,1,0:T(8,128)} %get-tuple-element.10.refs_2_, ...), custom_call_target="tpu_custom_call" | custom-call | tf_op jit(solution)/shard_map/pallas_call | solution.py:458

commit v5 on v4

--- a/solution.py
+++ b/solution.py
@@ -193,9 +193,12 @@
             x_all.at[r, rows_q, :], xd_send.at[r], xd_recv.at[r], to,
         )
 
-    for r in order:
-        back = (8 - r) % 8
-        direct(back, *ring(back)).start()
+    def send_x(slots):
+        for r in slots:
+            back = (8 - r) % 8
+            direct(back, *ring(back)).start()
+
+    send_x(turns)
 
     for copy in loads[3:]:
         copy.wait()
@@ -217,12 +220,10 @@
     def column(row):
         return jnp.transpose(jnp.broadcast_to(row, (HD, tokens)))
 
-    def block(key, value, key_pos, first, forwards):
-        visible = key_pos <= pos_row
+    def block(key, value, visible, which, sums, seen):
         key_t = jnp.transpose(key)
-        dk = jnp.zeros((tokens, HD), jnp.float32)
-        dv = jnp.zeros((tokens, HD), jnp.float32)
-        for i in range(heads):
+        dk, dv = sums
+        for i in which:
             cols = slice(i * HD, (i + 1) * HD)
             scores = jnp.dot(key, qt_ref[i], preferred_element_type=jnp.float32)
             probs = jnp.exp2(scores * (factor * LOG2E) - lse_low[i:i + 1, :])
@@ -233,13 +234,11 @@
             dv = dv + jnp.dot(probs, g_ref[0, :, cols], preferred_element_type=jnp.float32)
             dk = dk + jnp.dot(dscores, q_ref[0, :, cols], preferred_element_type=jnp.float32)
             dqt = jnp.dot(key_t, dscores, preferred_element_type=jnp.float32)
-            if first:
+            if i in seen:
+                dq_ref[0, :, cols] = jnp.transpose((dqt_ref[i] + dqt) * factor)
+            else:
                 dqt_ref[i] = dqt
-            else:
-                dq_ref[0, :, cols] = jnp.transpose((dqt_ref[i] + dqt) * factor)
-            if i in forwards:
-                forward_x(forwards[i])
-        return dk * factor, dv
+        return dk, dv
 
     def over_x(r):
         part = x_all.at[r, rows_q, :]
@@ -257,11 +256,16 @@
         over_x(order[n]).wait_recv()
         over_core(order[n]).start()
 
+    zero = jnp.zeros((tokens, HD), jnp.float32)
+    early, late = range(heads // 2), range(heads // 2, heads)
+    own_sees = column(pos_row)[:, 0:1] <= pos_row
+    own_sums = block(k_ref[0], v_ref[0], own_sees, early, (zero, zero), ())
     for copy in kv_copies:
         copy.wait_recv()
-    dk, dv = block(
-        kv_peer[0], kv_peer[1], column(pos_peer[0:1, :].astype(jnp.float32))[:, 0:1], True, {}
-    )
+    send_x(odd_turns)
+    peer_sees = column(pos_peer[0:1, :].astype(jnp.float32))[:, 0:1] <= pos_row
+    dk, dv = block(kv_peer[0], kv_peer[1], peer_sees, range(heads), (zero, zero), early)
+    dk = dk * factor
     part_copies = []
     for c in range(2):
         rows = slice(c * half, (c + 1) * half)
@@ -272,9 +276,8 @@
         )
         copy.start()
         part_copies.append(copy)
-    dk_own, dv_own = block(
-        k_ref[0], v_ref[0], column(pos_row)[:, 0:1], False, {0: 0, 2: 1, 4: 2, 6: 3}
-    )
+    dk_own, dv_own = block(k_ref[0], v_ref[0], own_sees, late, own_sums, late)
+    dk_own = dk_own * factor
     saves = [
         pltpu.make_async_copy(src, dst, save_sem.at[i])
         for i, (src, dst) in enumerate((
@@ -286,7 +289,7 @@
     up, down = {"dp": z + 1}, {"dp": z - 1}
 
     def pass_block(c, step, r, to_up, to_down):
-        rows = slice(c * half, (c + 1) * half)
+        rows = slice(c * quarter, (c + 1) * quarter)
         src = kv_all.at[r, rows, :]
         slots = ((r + 9 - 2 * y) % 8, (r + 2) % 8, (r + 6) % 8)
         copies = [
@@ -300,11 +303,13 @@
         return copies, to_up, to_down
 
     passed = []
-    for c in range(2):
-        rows = slice(c * half, (c + 1) * half)
-        part_copies[c].wait_recv()
-        dk = dk_own[rows] + part_recv[c, :, 0:HD].astype(jnp.float32)
-        dv = dv_own[rows] + part_recv[c, :, HD:].astype(jnp.float32)
+    for c in range(4):
+        rows = slice(c * quarter, (c + 1) * quarter)
+        if c % 2 == 0:
+            part_copies[c // 2].wait_recv()
+        there = slice(c % 2 * quarter, (c % 2 + 1) * quarter)
+        dk = dk_own[rows] + part_recv[c // 2, there, 0:HD].astype(jnp.float32)
+        dv = dv_own[rows] + part_recv[c // 2, there, HD:].astype(jnp.float32)
         dk_ref[0, rows, :] = dk
         dv_ref[0, rows, :] = dv
         kv_all[0, rows, 0:HD] = dk.astype(jnp.bfloat16)
@@ -312,15 +317,13 @@
         passed.append(pass_block(c, 0, 0, z < 3, z > 0))
 
     def arrived(c, r):
-        rows = slice(c * half, (c + 1) * half)
-        send(
-            kv_all.at[r, rows, :], kv_all.at[r, rows, :], g_send.at[c, 0, 0], g_recv.at[c, r], y_peer
-        ).wait_recv()
+        part = kv_all.at[r, pl.ds(c * quarter, quarter), :]
+        send(part, part, g_send.at[c, 0, 0], g_recv.at[c, r], y_peer).wait_recv()
 
     def forward_kv(step):
         r = turns[step - 1]
         rising = z >= r // 2
-        for c in range(2):
+        for c in range(4):
             arrived(c, r)
             passed.append(
                 pass_block(
@@ -338,40 +341,37 @@
         w_ref[...] += jnp.dot(xt_all[r], kv_all[r], preferred_element_type=jnp.float32)
 
     def add_odd(n):
-        arrived(0, odd_turns[n])
-        arrived(1, odd_turns[n])
+        for c in range(4):
+            arrived(c, odd_turns[n])
         add(odd_turns[n])
 
     saves[1].start()
     saves[2].start()
-    forward_x(4)
-    for n in (0, 1, 2):
-        forward_core(n)
+    for n in (1, 3, 5):
+        forward_x(n)
     own_x.wait()
     xt_all[0] = jnp.transpose(x_all[0])
     w_ref[...] = jnp.dot(xt_all[0], kv_all[0], preferred_element_type=jnp.float32)
     forward_kv(1)
-    forward_x(5)
-    forward_x(6)
-    forward_core(3)
+    for n in (0, 2, 4, 6):
+        forward_x(n)
+    for n in (1, 3, 5):
+        forward_core(n)
+    forward_kv(2)
+    turn_x(1)
+    add(turns[0])
+    turn_x(3)
+    add(turns[1])
+    forward_core(0)
+    forward_core(2)
+    turn_x(5)
+    forward_kv(3)
     forward_core(4)
-    for n in (0, 1, 2):
+    forward_core(6)
+    add(turns[2])
+    for n in (0, 2, 4, 6):
         turn_x(n)
-    forward_kv(2)
-    add(turns[0])
-    add_odd(0)
-    turn_x(3)
-    forward_core(5)
-    add(turns[1])
-    turn_x(4)
-    forward_kv(3)
-    forward_core(6)
-    add_odd(1)
-    turn_x(5)
-    add(turns[2])
-    add_odd(2)
-    turn_x(6)
-    add_odd(3)
+        add_odd(n // 2)
 
     saves[3].start()
     for copy in kv_copies + part_copies:
@@ -449,7 +449,7 @@
             dma((8,)), dma((8,)),
             dma((8,)), dma((8,)),
             dma((8,)), dma((8,)),
-            dma((2, 4, 3)), dma((2, 8)),
+            dma((4, 4, 3)), dma((4, 8)),
         ],
         compiler_params=pltpu.CompilerParams(
             collective_id=0, has_side_effects=True, vmem_limit_bytes=VMEM_BYTES

time: 44.5 us -> 46.2 us (1.038)
  Pallas kernels: 43.7 us -> 45.4 us
    pallas_call x1, Pallas kernels: 41.2 us -> 42.8 us  [fused(): pl.pallas_call(fused_kernel, out_shape=shapes, in_specs=[hbm] * 8, out_sp...]
where the time goes in v5:
time: 46.2 us; the launch traced here: 46 us
  Pallas kernels  45.4 us (98%)
  between operations  0.64 us (1%)
    pallas_call x1, Pallas kernels, fused(): pl.pallas_call(fused_kernel, out_shape=shapes, in_specs=[hbm] * 8, out_sp...  42.8 us
    pallas_call x1, Pallas kernels, fused(): pl.pallas_call(write_kernel, out_shape=shapes, in_specs=[hbm] * 4, out_sp...  2.53 us

profile of v5, /device:TPU:0, one launch (start us, length us, event | category | flops | bytes accessed | tf_op | source)
XLA Modules:
  0.0 46.0 jit_solution(1880837248568229840)
XLA Ops:
  0.6 42.8 %shard_map.111 = (f32[1,256,1024]{2,1,0:T(8,128)}, f32[1,256,128]{2,1,0:T(8,128)}, f32[1,256,128]{2,1,0:T(8,128)}, f32[640,256]{1,0:T(8,128)}) custom-call(bf16[1,256,5120]{2,1,0:T(8,128)(2,1)} %x_ref.1, bf16[1,256,1024]{2,1,0:T(8,128)(2,1)} %q_hbm.1, bf16[1,256,128]{2,1,0:T(8,128)(2,1)} %k_hbm.1, bf16[1,256,128]{2,1,0:T(8,128)(2,1)} %v_hbm.1, ...), custom_call_target="tpu_custom_call" | custom-call | tf_op jit(solution)/shard_map/pallas_call | solution.py:426
  43.5 2.5 %shard_map.112 = (f32[1,256,1024]{2,1,0:T(8,128)}, f32[1,256,128]{2,1,0:T(8,128)}, f32[1,256,128]{2,1,0:T(8,128)}, f32[640,256]{1,0:T(8,128)}) custom-call(f32[1,256,1024]{2,1,0:T(8,128)} %get-tuple-element.8.refs_0_, f32[1,256,128]{2,1,0:T(8,128)} %get-tuple-element.9.refs_1_, f32[1,256,128]{2,1,0:T(8,128)} %get-tuple-element.10.refs_2_, ...), custom_call_target="tpu_custom_call" | custom-call | tf_op jit(solution)/shard_map/pallas_call | solution.py:458

commit v6 on v5

--- a/solution.py
+++ b/solution.py
@@ -123,7 +123,7 @@
     dq_hbm, dk_hbm, dv_hbm, w_hbm,
     dq_ref, dk_ref, dv_ref, w_ref, save_sem,
     q_ref, k_ref, v_ref, o_ref, g_ref, lse_ref, pos_ref, load_sem,
-    kv_peer, pos_send, pos_peer, qt_ref, gt_ref, dqt_ref, xt_all, part_send, part_recv, kv_all, x_all,
+    kv_peer, pos_send, pos_peer, qt_ref, gt_ref, dqt_ref, wt_ref, part_send, part_recv, kv_all, x_all,
     local_sem, kv_send, kv_recv, part_ssem, part_rsem,
     xd_send, xd_recv, xx_send, xx_recv, xc_send, xc_recv, g_send, g_recv,
 ):
@@ -276,24 +276,26 @@
         )
         copy.start()
         part_copies.append(copy)
+    forward_x(1)
     dk_own, dv_own = block(k_ref[0], v_ref[0], own_sees, late, own_sums, late)
     dk_own = dk_own * factor
     saves = [
         pltpu.make_async_copy(src, dst, save_sem.at[i])
         for i, (src, dst) in enumerate((
-            (dq_ref, dq_hbm), (dk_ref, dk_hbm), (dv_ref, dv_hbm), (w_ref, w_hbm),
+            (dq_ref, dq_hbm), (dk_ref, dk_hbm), (dv_ref, dv_hbm),
         ))
     ]
     saves[0].start()
+    forward_x(3)
 
     up, down = {"dp": z + 1}, {"dp": z - 1}
 
     def pass_block(c, step, r, to_up, to_down):
-        rows = slice(c * quarter, (c + 1) * quarter)
-        src = kv_all.at[r, rows, :]
+        cols = slice(c * half, (c + 1) * half)
+        src = kv_all.at[r, :, cols]
         slots = ((r + 9 - 2 * y) % 8, (r + 2) % 8, (r + 6) % 8)
         copies = [
-            send(src, kv_all.at[slot, rows, :], g_send.at[c, step, d], g_recv.at[c, slot], to)
+            send(src, kv_all.at[slot, :, cols], g_send.at[c, step, d], g_recv.at[c, slot], to)
             for d, (slot, to) in enumerate(zip(slots, (y_peer, up, down)))
         ]
         if to_up is not None:
@@ -303,27 +305,25 @@
         return copies, to_up, to_down
 
     passed = []
-    for c in range(4):
-        rows = slice(c * quarter, (c + 1) * quarter)
-        if c % 2 == 0:
-            part_copies[c // 2].wait_recv()
-        there = slice(c % 2 * quarter, (c % 2 + 1) * quarter)
-        dk = dk_own[rows] + part_recv[c // 2, there, 0:HD].astype(jnp.float32)
-        dv = dv_own[rows] + part_recv[c // 2, there, HD:].astype(jnp.float32)
+    for c in range(2):
+        rows = slice(c * half, (c + 1) * half)
+        part_copies[c].wait_recv()
+        dk = dk_own[rows] + part_recv[c, :, 0:HD].astype(jnp.float32)
+        dv = dv_own[rows] + part_recv[c, :, HD:].astype(jnp.float32)
         dk_ref[0, rows, :] = dk
         dv_ref[0, rows, :] = dv
-        kv_all[0, rows, 0:HD] = dk.astype(jnp.bfloat16)
-        kv_all[0, rows, HD:] = dv.astype(jnp.bfloat16)
+        kv_all[0, 0:HD, rows] = jnp.transpose(dk).astype(jnp.bfloat16)
+        kv_all[0, HD:, rows] = jnp.transpose(dv).astype(jnp.bfloat16)
         passed.append(pass_block(c, 0, 0, z < 3, z > 0))
 
     def arrived(c, r):
-        part = kv_all.at[r, pl.ds(c * quarter, quarter), :]
+        part = kv_all.at[r, :, pl.ds(c * half, half)]
         send(part, part, g_send.at[c, 0, 0], g_recv.at[c, r], y_peer).wait_recv()
 
     def forward_kv(step):
         r = turns[step - 1]
         rising = z >= r // 2
-        for c in range(4):
+        for c in range(2):
             arrived(c, r)
             passed.append(
                 pass_block(
@@ -333,47 +333,48 @@
                 )
             )
 
-    def turn_x(n):
-        over_core(order[n]).wait_recv()
-        xt_all[order[n]] = jnp.transpose(x_all[order[n]])
-
-    def add(r):
-        w_ref[...] += jnp.dot(xt_all[r], kv_all[r], preferred_element_type=jnp.float32)
-
-    def add_odd(n):
-        for c in range(4):
-            arrived(c, odd_turns[n])
-        add(odd_turns[n])
+    def add(n):
+        r = order[n]
+        over_core(r).wait_recv()
+        if n % 2 == 0:
+            arrived(0, r)
+            arrived(1, r)
+        wt_ref[...] += jnp.dot(kv_all[r], x_all[r], preferred_element_type=jnp.float32)
 
     saves[1].start()
     saves[2].start()
-    for n in (1, 3, 5):
+    for n in (0, 5, 2):
         forward_x(n)
+    forward_core(1)
+    forward_core(3)
     own_x.wait()
-    xt_all[0] = jnp.transpose(x_all[0])
-    w_ref[...] = jnp.dot(xt_all[0], kv_all[0], preferred_element_type=jnp.float32)
+    wt_ref[...] = jnp.dot(kv_all[0], x_all[0], preferred_element_type=jnp.float32)
+    forward_x(4)
     forward_kv(1)
-    for n in (0, 2, 4, 6):
-        forward_x(n)
-    for n in (1, 3, 5):
+    forward_x(6)
+    for n in (0, 5, 2):
         forward_core(n)
+    add(1)
     forward_kv(2)
-    turn_x(1)
-    add(turns[0])
-    turn_x(3)
-    add(turns[1])
-    forward_core(0)
-    forward_core(2)
-    turn_x(5)
+    forward_core(4)
+    add(0)
+    add(3)
     forward_kv(3)
-    forward_core(4)
     forward_core(6)
-    add(turns[2])
-    for n in (0, 2, 4, 6):
-        turn_x(n)
-        add_odd(n // 2)
-
-    saves[3].start()
+    for n in (2, 5, 4):
+        add(n)
+    r = order[6]
+    over_core(r).wait_recv()
+    arrived(0, r)
+    arrived(1, r)
+    for n in range(width // HD):
+        part = slice(n * HD, (n + 1) * HD)
+        term = jnp.dot(kv_all[r], x_all[r, :, part], preferred_element_type=jnp.float32)
+        w_ref[part, :] = jnp.transpose(wt_ref[:, part] + term)
+        saves.append(
+            pltpu.make_async_copy(w_ref.at[part, :], w_hbm.at[part, :], save_sem.at[3 + n])
+        )
+        saves[-1].start()
     for copy in kv_copies + part_copies:
         copy.wait_send()
     for r in range(1, 8):
@@ -429,7 +430,7 @@
         in_specs=[hbm] * 8,
         out_specs=(hbm,) * 4,
         scratch_shapes=[pltpu.VMEM(a.shape, a.dtype) for a in shapes] + [
-            dma((4,)),
+            dma((3 + width // HD,)),
         ] + [pltpu.VMEM(a.shape, a.dtype) for a in args[1:]] + [
             dma((7,)),
             pltpu.VMEM((2, tokens, HD), bf16),
@@ -438,7 +439,7 @@
             pltpu.VMEM((queries.shape[2] // HD, HD, tokens), bf16),
             pltpu.VMEM((queries.shape[2] // HD, HD, tokens), bf16),
             pltpu.VMEM((queries.shape[2] // HD, HD, tokens), f32),
-            pltpu.VMEM((8, width, tokens), bf16),
+            pltpu.VMEM((2 * HD, width), f32),
             pltpu.VMEM((2, tokens // 2, 2 * HD), bf16),
             pltpu.VMEM((2, tokens // 2, 2 * HD), bf16),
             pltpu.VMEM((8, tokens, 2 * HD), bf16),
@@ -449,7 +450,7 @@
             dma((8,)), dma((8,)),
             dma((8,)), dma((8,)),
             dma((8,)), dma((8,)),
-            dma((4, 4, 3)), dma((4, 8)),
+            dma((2, 4, 3)), dma((2, 8)),
         ],
         compiler_params=pltpu.CompilerParams(
             collective_id=0, has_side_effects=True, vmem_limit_bytes=VMEM_BYTES

time: 46.2 us -> 44.6 us (0.965)
  Pallas kernels: 45.4 us -> 43.8 us
    pallas_call x1, Pallas kernels: 42.8 us -> 41.3 us  [fused(): pl.pallas_call(fused_kernel, out_shape=shapes, in_specs=[hbm] * 8, out_sp...]
where the time goes in v6:
time: 44.6 us; the launch traced here: 44.5 us
  Pallas kernels  43.8 us (98%)
  between operations  0.64 us (1%)
    pallas_call x1, Pallas kernels, fused(): pl.pallas_call(fused_kernel, out_shape=shapes, in_specs=[hbm] * 8, out_sp...  41.3 us
    pallas_call x1, Pallas kernels, fused(): pl.pallas_call(write_kernel, out_shape=shapes, in_specs=[hbm] * 4, out_sp...  2.53 us

profile of v6, /device:TPU:0, one launch (start us, length us, event | category | flops | bytes accessed | tf_op | source)
XLA Modules:
  0.0 44.5 jit_solution(18223463672378866552)
XLA Ops:
  0.6 41.3 %shard_map.111 = (f32[1,256,1024]{2,1,0:T(8,128)}, f32[1,256,128]{2,1,0:T(8,128)}, f32[1,256,128]{2,1,0:T(8,128)}, f32[640,256]{1,0:T(8,128)}) custom-call(bf16[1,256,5120]{2,1,0:T(8,128)(2,1)} %x_ref.1, bf16[1,256,1024]{2,1,0:T(8,128)(2,1)} %q_hbm.1, bf16[1,256,128]{2,1,0:T(8,128)(2,1)} %k_hbm.1, bf16[1,256,128]{2,1,0:T(8,128)(2,1)} %v_hbm.1, ...), custom_call_target="tpu_custom_call" | custom-call | tf_op jit(solution)/shard_map/pallas_call | solution.py:427
  41.9 2.5 %shard_map.112 = (f32[1,256,1024]{2,1,0:T(8,128)}, f32[1,256,128]{2,1,0:T(8,128)}, f32[1,256,128]{2,1,0:T(8,128)}, f32[640,256]{1,0:T(8,128)}) custom-call(f32[1,256,1024]{2,1,0:T(8,128)} %get-tuple-element.8.refs_0_, f32[1,256,128]{2,1,0:T(8,128)} %get-tuple-element.9.refs_1_, f32[1,256,128]{2,1,0:T(8,128)} %get-tuple-element.10.refs_2_, ...), custom_call_target="tpu_custom_call" | custom-call | tf_op jit(solution)/shard_map/pallas_call | solution.py:459

commit v7 on v6

--- a/solution.py
+++ b/solution.py
@@ -198,7 +198,7 @@
             back = (8 - r) % 8
             direct(back, *ring(back)).start()
 
-    send_x(turns)
+    send_x(turns[::-1])
 
     for copy in loads[3:]:
         copy.wait()
@@ -262,7 +262,7 @@
     own_sums = block(k_ref[0], v_ref[0], own_sees, early, (zero, zero), ())
     for copy in kv_copies:
         copy.wait_recv()
-    send_x(odd_turns)
+    send_x(odd_turns[::-1])
     peer_sees = column(pos_peer[0:1, :].astype(jnp.float32))[:, 0:1] <= pos_row
     dk, dv = block(kv_peer[0], kv_peer[1], peer_sees, range(heads), (zero, zero), early)
     dk = dk * factor
@@ -277,6 +277,7 @@
         copy.start()
         part_copies.append(copy)
     forward_x(1)
+    forward_x(3)
     dk_own, dv_own = block(k_ref[0], v_ref[0], own_sees, late, own_sums, late)
     dk_own = dk_own * factor
     saves = [
@@ -286,7 +287,7 @@
         ))
     ]
     saves[0].start()
-    forward_x(3)
+    forward_x(5)
 
     up, down = {"dp": z + 1}, {"dp": z - 1}
 
@@ -343,25 +344,23 @@
 
     saves[1].start()
     saves[2].start()
-    for n in (0, 5, 2):
-        forward_x(n)
     forward_core(1)
     forward_core(3)
     own_x.wait()
     wt_ref[...] = jnp.dot(kv_all[0], x_all[0], preferred_element_type=jnp.float32)
-    forward_x(4)
+    forward_x(0)
     forward_kv(1)
-    forward_x(6)
-    for n in (0, 5, 2):
-        forward_core(n)
+    for n in (2, 4, 6):
+        forward_x(n)
+    forward_core(5)
     add(1)
     forward_kv(2)
-    forward_core(4)
-    add(0)
+    forward_core(0)
     add(3)
     forward_kv(3)
-    forward_core(6)
-    for n in (2, 5, 4):
+    for n in (2, 4, 6):
+        forward_core(n)
+    for n in (5, 0, 2, 4):
         add(n)
     r = order[6]
     over_core(r).wait_recv()

time: 44.6 us -> 41.5 us (0.930)
  Pallas kernels: 43.8 us -> 40.7 us
    pallas_call x1, Pallas kernels: 41.3 us -> 38.2 us  [fused(): pl.pallas_call(fused_kernel, out_shape=shapes, in_specs=[hbm] * 8, out_sp...]
where the time goes in v7:
time: 41.5 us; the launch traced here: 41.3 us
  Pallas kernels  40.7 us (98%)
  between operations  0.64 us (2%)
    pallas_call x1, Pallas kernels, fused(): pl.pallas_call(fused_kernel, out_shape=shapes, in_specs=[hbm] * 8, out_sp...  38.2 us
    pallas_call x1, Pallas kernels, fused(): pl.pallas_call(write_kernel, out_shape=shapes, in_specs=[hbm] * 4, out_sp...  2.53 us

profile of v7, /device:TPU:0, one launch (start us, length us, event | category | flops | bytes accessed | tf_op | source)
XLA Modules:
  0.0 41.3 jit_solution(3308196876299241902)
XLA Ops:
  0.6 38.2 %shard_map.111 = (f32[1,256,1024]{2,1,0:T(8,128)}, f32[1,256,128]{2,1,0:T(8,128)}, f32[1,256,128]{2,1,0:T(8,128)}, f32[640,256]{1,0:T(8,128)}) custom-call(bf16[1,256,5120]{2,1,0:T(8,128)(2,1)} %x_ref.1, bf16[1,256,1024]{2,1,0:T(8,128)(2,1)} %q_hbm.1, bf16[1,256,128]{2,1,0:T(8,128)(2,1)} %k_hbm.1, bf16[1,256,128]{2,1,0:T(8,128)(2,1)} %v_hbm.1, ...), custom_call_target="tpu_custom_call" | custom-call | tf_op jit(solution)/shard_map/pallas_call | solution.py:426
  38.8 2.5 %shard_map.112 = (f32[1,256,1024]{2,1,0:T(8,128)}, f32[1,256,128]{2,1,0:T(8,128)}, f32[1,256,128]{2,1,0:T(8,128)}, f32[640,256]{1,0:T(8,128)}) custom-call(f32[1,256,1024]{2,1,0:T(8,128)} %get-tuple-element.8.refs_0_, f32[1,256,128]{2,1,0:T(8,128)} %get-tuple-element.9.refs_1_, f32[1,256,128]{2,1,0:T(8,128)} %get-tuple-element.10.refs_2_, ...), custom_call_target="tpu_custom_call" | custom-call | tf_op jit(solution)/shard_map/pallas_call | solution.py:458

commit v8 on v7

--- a/solution.py
+++ b/solution.py
@@ -198,7 +198,7 @@
             back = (8 - r) % 8
             direct(back, *ring(back)).start()
 
-    send_x(turns[::-1])
+    send_x(turns[::-1] + tuple(odd_turns[:1:-1]))
 
     for copy in loads[3:]:
         copy.wait()
@@ -262,7 +262,7 @@
     own_sums = block(k_ref[0], v_ref[0], own_sees, early, (zero, zero), ())
     for copy in kv_copies:
         copy.wait_recv()
-    send_x(odd_turns[::-1])
+    send_x(odd_turns[1::-1])
     peer_sees = column(pos_peer[0:1, :].astype(jnp.float32))[:, 0:1] <= pos_row
     dk, dv = block(kv_peer[0], kv_peer[1], peer_sees, range(heads), (zero, zero), early)
     dk = dk * factor
@@ -357,8 +357,9 @@
     forward_kv(2)
     forward_core(0)
     add(3)
+    forward_core(2)
     forward_kv(3)
-    for n in (2, 4, 6):
+    for n in (4, 6):
         forward_core(n)
     for n in (5, 0, 2, 4):
         add(n)

time: 41.5 us -> 42 us (1.012)
  Pallas kernels: 40.7 us -> 41.2 us
    pallas_call x1, Pallas kernels: 38.2 us -> 38.6 us  [fused(): pl.pallas_call(fused_kernel, out_shape=shapes, in_specs=[hbm] * 8, out_sp...]
where the time goes in v8:
time: 42 us; the launch traced here: 41.8 us
  Pallas kernels  41.2 us (98%)
  between operations  0.64 us (2%)
    pallas_call x1, Pallas kernels, fused(): pl.pallas_call(fused_kernel, out_shape=shapes, in_specs=[hbm] * 8, out_sp...  38.6 us
    pallas_call x1, Pallas kernels, fused(): pl.pallas_call(write_kernel, out_shape=shapes, in_specs=[hbm] * 4, out_sp...  2.53 us

profile of v8, /device:TPU:0, one launch (start us, length us, event | category | flops | bytes accessed | tf_op | source)
XLA Modules:
  0.0 41.8 jit_solution(10002850657572893126)
XLA Ops:
  0.6 38.6 %shard_map.111 = (f32[1,256,1024]{2,1,0:T(8,128)}, f32[1,256,128]{2,1,0:T(8,128)}, f32[1,256,128]{2,1,0:T(8,128)}, f32[640,256]{1,0:T(8,128)}) custom-call(bf16[1,256,5120]{2,1,0:T(8,128)(2,1)} %x_ref.1, bf16[1,256,1024]{2,1,0:T(8,128)(2,1)} %q_hbm.1, bf16[1,256,128]{2,1,0:T(8,128)(2,1)} %k_hbm.1, bf16[1,256,128]{2,1,0:T(8,128)(2,1)} %v_hbm.1, ...), custom_call_target="tpu_custom_call" | custom-call | tf_op jit(solution)/shard_map/pallas_call | solution.py:427
  39.3 2.5 %shard_map.112 = (f32[1,256,1024]{2,1,0:T(8,128)}, f32[1,256,128]{2,1,0:T(8,128)}, f32[1,256,128]{2,1,0:T(8,128)}, f32[640,256]{1,0:T(8,128)}) custom-call(f32[1,256,1024]{2,1,0:T(8,128)} %get-tuple-element.8.refs_0_, f32[1,256,128]{2,1,0:T(8,128)} %get-tuple-element.9.refs_1_, f32[1,256,128]{2,1,0:T(8,128)} %get-tuple-element.10.refs_2_, ...), custom_call_target="tpu_custom_call" | custom-call | tf_op jit(solution)/shard_map/pallas_call | solution.py:459
